TPU v7x, 32 devices: a whole 2x2x4 slice. The times are simulated.
32 devices in a mesh: mel: 4 (over y, x), tm: 8 (over z, core).
Axes of the slice: x: 2, y: 2, z: 4, core: 2. Of those that a mesh axis runs over, the one named last changes fastest.
Arguments:
- spectrum: bfloat16 [1, 64, 2048], P(None, 'mel', 'tm'), may hold values from -25 to 40
- clip_bounds: int32 [1, 4], replicated, may hold values from 0 to 2048, as said below
- kernel_one: bfloat16 [64, 3, 3], replicated, may hold values from -2 to 2
- gain_one: float32 [64], replicated, may hold values from 0.5 to 1.5
- bias_one: float32 [64], replicated, may hold values from -3 to 3
- kernel_two: bfloat16 [64, 64, 3, 3], replicated, may hold values from -0.25 to 0.25
- gain_two: float32 [64], replicated, may hold values from 0.5 to 1.5
- bias_two: float32 [64], replicated, may hold values from -3 to 3
- pooled_grad: bfloat16 [1, 64, 32, 1024], P(None, None, 'mel', 'tm'), may hold values from -14 to 19
Outputs:
- pooled: bfloat16 [1, 64, 32, 1024], P(None, None, 'mel', 'tm')
- spectrum_grad: float32 [1, 64, 2048], P(None, 'mel', 'tm')
- kernel_one_grad: float32 [64, 3, 3], replicated
- gain_one_grad: float32 [64], replicated
- bias_one_grad: float32 [64], replicated
- kernel_two_grad: float32 [64, 64, 3, 3], replicated
- gain_two_grad: float32 [64], replicated
- bias_two_grad: float32 [64], replicated
Inputs may be any that keep to these rules, and one draw needn't show every extreme that they name: `clip_bounds`: in each row the entries rise strictly and are even; entry 0 is 0, entries 0 to 2 are the clips' first frames and entry 3 the end of the last clip; frames from there on are padding.
All inputs are finite; a program needn't handle non-finite values.
Results may differ from a plain program's by a relative error of at most 0.0056.
Values may be sent and summed in bfloat16 or wider, within the bound.
No kernel may reach another device: no remote copies, remote signals or barrier semaphores. Data moves between devices by JAX's collectives and lax.ppermute only.
A program may use at most 64 MiB of HBM per device.

v0:
```python
import math

import jax
import jax.numpy as jnp
from jax import lax
from jax.experimental import pallas as pl
from jax.experimental.pallas import tpu as pltpu
from jax.sharding import PartitionSpec as P

F32 = jnp.float32
BF16 = jnp.bfloat16
AXES = ("mel", "tm")
EXACT = lax.Precision.HIGHEST
RIM = 128
BAND = 24
MEL_ROWS = 16
FIRST = 24
SUMS, EDGES, COLUMNS = 16, 19, 23
SIDE = 96
TAPS = 576
SECOND = 8


def iota(shape, dim):
    return lax.broadcasted_iota(jnp.int32, shape, dim)


def dot(a, b, over=((1,), (0,)), precision=None):
    return lax.dot_general(a, b, (over, ((), ())), precision=precision, preferred_element_type=F32)


def to_column(lanes, count, start=0):
    shape = (count, lanes.shape[1])
    return jnp.sum(jnp.where(iota(shape, 1) == iota(shape, 0) + start, lanes, 0.0), axis=1, keepdims=True)


def to_lanes(column, start=0, width=128):
    shape = (column.shape[0], width)
    return jnp.sum(jnp.where(iota(shape, 1) == iota(shape, 0) + start, column, 0.0), axis=0, keepdims=True)


def halves(v):
    total = v[:, :128]
    for n in range(128, v.shape[1], 128):
        total = total + v[:, n : n + 128]
    return total


def frame_masks(bounds, frames):
    last = bounds.shape[1] - 1

    def living(f):
        return (f >= 0) & (f < bounds[0, last])

    def paired(f):
        both = living(f) & living(f + 1)
        for k in range(1, last):
            both = both & (f + 1 != bounds[0, k])
        return both

    return tuple(m.astype(F32) for m in (living(frames), paired(frames - 1), paired(frames)))


def row_valid(row, rows):
    mel = lax.axis_index("mel") * rows + row
    return ((mel >= 0) & (mel < lax.axis_size("mel") * rows)).astype(F32)


def start_all(*pairs, sems):
    copies = [pltpu.make_async_copy(src, dst, sems.at[n]) for n, (src, dst) in enumerate(pairs)]
    for copy in copies:
        copy.start()
    return copies


def wait_all(copies):
    for copy in copies:
        copy.wait()


def shifted_frames(value, behind, ahead):
    wide = value.shape[1]
    return pltpu.roll(value, 1, 1) * behind, pltpu.roll(value, wide - 1, 1) * ahead


def three_parts(v):
    high = lax.reduce_precision(v, 8, 7)
    mid = lax.reduce_precision(v - high, 8, 7)
    return high, mid, v - high - mid


def share_of(devices, chan):
    return -(-chan // devices)


def pack(spec_hbm, grad_hbm, bounds_hbm, out, own, spec, masks, bounds, edges, rows_out, sems):
    copies = start_all((bounds_hbm, bounds), (spec_hbm, spec), (grad_hbm, own), sems=sems)
    copies[0].wait()
    wide = masks.shape[1]
    frame_dev = wide - RIM
    devices = out.shape[0]
    rows = MEL_ROWS
    lane = iota((1, wide), 1)
    frames = lax.axis_index("tm") * frame_dev + jnp.where(lane < frame_dev + RIM // 2, lane, lane - wide)
    last = bounds.shape[1] - 1
    pixels = (bounds[0, last] * (lax.axis_size("mel") * rows)).astype(F32)
    found = frame_masks(bounds, frames)
    masks[...] = jnp.concatenate(
        list(found) + [jnp.full((1, wide), 1.0) * pixels, jnp.zeros((4, wide), F32)], axis=0
    )
    usable, behind, ahead = (m[:, :frame_dev] for m in found)
    copies[1].wait()
    x = spec[0].astype(F32) * usable
    lane = iota((1, frame_dev), 1)
    row = iota((rows, 1), 0)
    inner = jnp.where((lane > 0) & (lane < frame_dev - 1), usable, 0.0)
    number = (rows - 2) * jnp.sum(inner, axis=1, keepdims=True)
    inner = inner * ((row > 0) & (row < rows - 1)).astype(F32)
    centre = jnp.sum(jnp.sum(x, axis=0, keepdims=True), axis=1, keepdims=True)
    centre = centre / (rows * jnp.maximum(jnp.sum(usable, axis=1, keepdims=True), 1.0))
    centre = lax.reduce_precision(centre, 8, 7)
    shifted = [pltpu.roll(x, 1, 1) * behind, x, pltpu.roll(x, frame_dev - 1, 1) * ahead]
    taps = [pltpu.roll(v, (1 - i) % rows, 0) if i != 1 else v for i in range(3) for v in shifted]
    features = feature_rows(centre, (taps, inner))
    lane = iota((1, 128), 1)
    features = jnp.where(lane == 90, centre, jnp.where(lane == 91, number, features))
    pick = iota((8, frame_dev), 0)
    column = jnp.where(pick < 4, pick, frame_dev - 8 + pick)
    strip = dot((iota((8, frame_dev), 1) == column).astype(BF16), x.astype(BF16), ((1,), (1,)))
    lane = iota((8, 128), 1)
    repeat = (iota((rows, 128), 1) % rows == iota((rows, 128), 0)).astype(BF16)
    strip = jnp.where(lane // rows == iota((8, 128), 0), dot(strip.astype(BF16), repeat), 0.0)
    strip = jnp.sum(strip, axis=0, keepdims=True)

    def put(n, value):
        rows_out[pl.ds(n, devices, stride=FIRST), :] = jnp.broadcast_to(value, (devices, 128))

    near = jnp.concatenate([x[0:4], x[rows - 4 :]], axis=0)
    near = jnp.concatenate([near[:, :128], near[:, 128:]], axis=0)
    for d in range(devices):
        rows_out[FIRST * d : FIRST * d + 16, :] = near
    put(COLUMNS, strip)
    copies[2].wait()
    _, chan, many, half = own.shape
    share = share_of(devices, chan)
    holders = chan // share
    g = own[0].astype(F32)
    edges[0:chan] = g[:, 0, :]
    edges[chan:] = g[:, many - 1, :]

    def spread_out(v):
        if holders < devices:
            v = jnp.concatenate([v, jnp.zeros((devices - holders, 128), F32)], axis=0)
        return v

    for n in range(share):
        put(EDGES + n, spread_out(edges[n * holders : (n + 1) * holders, :]))
        put(EDGES + share + n, spread_out(edges[chan + n * holders : chan + (n + 1) * holders, :]))
    for n in range(2 * share, COLUMNS - EDGES):
        put(EDGES + n, jnp.zeros((1, 128), F32))
    end = iota((8, half), 0)
    at = iota((8, half), 1)
    ends = ((end == 0) & (at == 0)) | ((end == 1) & (at == half - 1))
    columns = dot(ends.astype(BF16), g.reshape(chan * many, half).astype(BF16), ((1,), (1,)))
    group = 128 // many
    source = iota((128, 128), 0)
    lane = iota((group, 128), 1)
    mine = lane // many == iota((group, 128), 0)
    parts = three_parts(features)
    for n in range(2):
        side = jnp.zeros((holders, 128), F32)
        for m in range(share):
            move = (iota((128, 128), 1) == SIDE + many * m + source % many).astype(BF16)
            first = m * holders * many // 128
            block = [columns[n : n + 1, 128 * q : 128 * (q + 1)] for q in range(first, first + holders * many // 128)]
            block = jnp.concatenate([jnp.where(mine, v, 0.0) for v in block], axis=0)
            side = side + dot(block.astype(BF16), move)
        put(SUMS + n, spread_out(side) + parts[n])
    put(SUMS + 2, parts[2])
    out[...] = rows_out[...].reshape(out.shape).astype(BF16)


def weights(own, bounds_hbm, k2_hbm, k1_hbm, gain_one_hbm, bias_one_hbm, gain_two_hbm, bias_two_hbm,
            wf, wb, w1, ws_hbm, pairs, singles, k1t, params, all_masks, edge_masks, twice, own_rows,
            k2, k1, vectors, bounds, ws, temp, sems):
    loads = start_all(
        (bounds_hbm, bounds),
        (k2_hbm, k2),
        (k1_hbm, k1),
        (gain_one_hbm, vectors.at[0]),
        (bias_one_hbm, vectors.at[1]),
        (gain_two_hbm, vectors.at[2]),
        (bias_two_hbm, vectors.at[3]),
        sems=sems,
    )
    _, many, count, half = own.shape
    temp[...] = own[0].astype(F32).reshape(many * count, half)
    for r in range(count):
        own_rows[r * many : (r + 1) * many] = temp[pl.ds(r, many, stride=count), :].astype(BF16)
    wait_all(loads)
    chan = k2.shape[1]
    span = wf.shape[1]
    taps = [k2[t].astype(F32) for t in range(9)]
    rest = jnp.zeros((chan, span - 9 * chan), F32)
    forward = jnp.concatenate(taps + [rest], axis=1)
    backward = jnp.concatenate([taps[8 - t].T for t in range(9)] + [rest], axis=1)
    for r in range(wb.shape[0] // chan):
        at = slice(r * chan, (r + 1) * chan)
        wb[at] = (pltpu.roll(backward, 3 * chan * r, 1) if r else backward).astype(BF16)
    full = jnp.concatenate([k1[n].astype(F32) for n in range(3)] + [jnp.zeros((7, chan), F32)], axis=0)
    low = [
        jnp.concatenate([full[3 * (2 - a) + 2 - b : 3 * (2 - a) + 3 - b] for a in range(3)], axis=1)
        for b in range(3)
    ]
    rest = jnp.zeros((1, ws.shape[1] - 3 * chan), F32)
    for b in range(3):
        base = jnp.concatenate([low[b], rest], axis=1)
        many = ws.shape[0] // 3
        rolled = [pltpu.roll(base, chan * m, 1) if m else base for m in range(many)]
        ws[many * b : many * (b + 1)] = jnp.concatenate(rolled, axis=0).astype(BF16)
    store_ws = pltpu.make_async_copy(ws, ws_hbm, sems.at[7])
    store_ws.start()
    count, frame_dev = all_masks.shape[0] // 3, all_masks.shape[1]
    frames = iota((count, frame_dev), 0) * frame_dev + iota((count, frame_dev), 1)
    for n, mask in enumerate(frame_masks(bounds, frames)):
        all_masks[n * count : (n + 1) * count] = mask
    q = iota(edge_masks.shape, 0)
    lane = iota(edge_masks.shape, 1)
    k = q % 8
    frames = (q // 8) * frame_dev + jnp.where(k < 4, k, k + frame_dev - 8)
    living, behind, ahead = frame_masks(bounds, frames)
    living = jnp.where((k == 0) | (k == 7), living, 0.0)
    edge_masks[...] = jnp.where(lane == 0, living, jnp.where(lane == 1, behind, jnp.where(lane == 2, ahead, 0.0)))
    params[...] = jnp.concatenate(
        [vectors[n] for n in range(4)] + [jnp.zeros((4, chan), F32)], axis=0
    )
    tap = iota((16, 128), 0)
    lane = iota((16, 128), 1)
    i = (tap * 11) >> 5
    ninth = (lane * 57) >> 9
    to_band = (lane == BAND * (tap - 3 * i) + i) & (tap < 9)
    to_left = (ninth == tap) & (tap < 9)
    to_right = (lane - 9 * ninth == tap) & (lane < 81)
    to_single = (lane == 81 + tap) & (tap < 9)
    source = iota((128, 128), 0) - 81
    lane = iota((128, 128), 1)
    ninth = (lane * 57) >> 9
    inside = (source >= 0) & (source < 9) & (lane < 81)
    twice[...] = jnp.where(inside, (source == ninth).astype(F32) + (source == lane - 9 * ninth).astype(F32), 0.0)
    for r in range(wf.shape[0] // chan):
        at = slice(r * chan, (r + 1) * chan)
        wf[at] = (pltpu.roll(forward, 3 * chan * r, 1) if r else forward).astype(BF16)
    k1t[...] = full
    k = full.astype(BF16)
    lanes = [dot(k, select.astype(BF16), ((0,), (0,))) for select in (to_band, to_left, to_right, to_single)]
    pairs[...] = lanes[1] * lanes[2]
    singles[...] = lanes[3]
    for m in range(w1.shape[0] // chan):
        w1[m * chan : (m + 1) * chan] = (pltpu.roll(lanes[0], m, 1) if m else lanes[0]).astype(BF16)
    store_ws.wait()


def feature_rows(centre, *parts):
    def folded(v):
        return jnp.sum(halves(v), axis=0, keepdims=True)

    rows = [jnp.zeros((1, 128), F32)] * 96
    for taps, weight in parts:
        z = [tap - centre for tap in taps]
        for s in range(9):
            left = z[s] * weight
            rows[81 + s] = rows[81 + s] + folded(left)
            for t in range(s, 9):
                rows[9 * s + t] = rows[9 * t + s] = rows[9 * s + t] + folded(left * z[t])
    return to_lanes(jnp.sum(jnp.concatenate(rows, axis=0), axis=1, keepdims=True))


def summed_blocks(ref, devices, by=1):
    block = ref.shape[0] // devices
    period = max(8 // math.gcd(block, 8), by)
    step = period * block
    total = ref[0:step, :]
    for at in range(step, ref.shape[0], step):
        total = total + ref[at : at + step, :]
    results = []
    for first in range(by):
        result = total[first * block : (first + 1) * block]
        for n in range(first + by, period, by):
            result = result + total[n * block : (n + 1) * block]
        results.append(result)
    return results if by > 1 else results[0]


def moved_rows(v, step):
    if step == 0:
        return v
    count = v.shape[0]
    if abs(step) >= count:
        return jnp.zeros_like(v)
    zero = jnp.zeros((abs(step), v.shape[1]), v.dtype)
    if step > 0:
        return jnp.concatenate([zero, v[: count - step]], axis=0)
    return jnp.concatenate([v[-step:], zero], axis=0)


def silu_halves(h):
    t = jnp.tanh(h)
    one = 1.0 + t
    return h * one, one * (1.0 + h * (1.0 - t))


def act_row(act, r, low, low_masks):
    low = low * low_masks[0]
    chan = low.shape[0]
    for n, v in enumerate((low,) + shifted_frames(low, *low_masks[1:])):
        at = (3 * r + (1, 0, 2)[n]) * chan
        act[at : at + chan, :] = v


def forward_one(recv, spec, pairs, singles, twice, w1, wf, params, masks, all_masks, edge_masks,
                pre_two, payload, act, x3, stats, features_out, pre_one, got, strips, halo, rows_out):
    devices = recv.shape[0]
    n_mel, count = lax.axis_size("mel"), lax.axis_size("tm")
    rows = MEL_ROWS
    mels = n_mel * rows
    wide = masks.shape[1]
    frame_dev = wide - RIM
    chan = params.shape[1]
    me_m, me_t = lax.axis_index("mel"), lax.axis_index("tm")
    usable, behind, ahead = (masks[n : n + 1] for n in range(3))
    total = masks[3:4, 0:1]
    got[...] = recv[...].astype(F32).reshape(devices * FIRST, 128)

    def every(n):
        return got[pl.ds(n, devices, stride=FIRST), :]

    lane = iota((count, 128), 1)
    bands = [got[pl.ds(FIRST * k * count + COLUMNS, count, stride=FIRST), :] for k in range(n_mel)]
    for c in range(8):
        column = jnp.zeros((count, 128), F32)
        for k, band in enumerate(bands):
            part = jnp.where(lane // rows == c, band, 0.0)
            column = column + (pltpu.roll(part, rows * (k - c) % 128, 1) if k != c else part)
        strips[pl.ds(c, count, stride=8), :] = column
    at = pl.multiple_of(FIRST * (jnp.maximum(me_m - 1, 0) * count + me_t), 8)
    above = got[pl.ds(at, 16), :] * (me_m > 0).astype(F32)
    at = pl.multiple_of(FIRST * (jnp.minimum(me_m + 1, n_mel - 1) * count + me_t), 8)
    below = got[pl.ds(at, 16), :] * (me_m < n_mel - 1).astype(F32)
    above = jnp.concatenate([above[4:8], above[12:16]], axis=1)
    below = jnp.concatenate([below[0:4], below[8:12]], axis=1)
    own = spec[0].astype(F32) * usable[:, :frame_dev]
    at = pl.multiple_of(8 * jnp.minimum(me_t + 1, count - 1), 8)
    after = strips[pl.ds(at, 8), :][:, :mels] * (me_t + 1 < count).astype(F32)
    at = pl.multiple_of(8 * jnp.maximum(me_t - 1, 0), 8)
    before = strips[pl.ds(at, 8), :][:, :mels] * (me_t > 0).astype(F32)
    sides = jnp.concatenate([after[0:4], before[4:8], jnp.zeros((8, mels), F32)], axis=0).astype(BF16)
    side = iota((16, RIM), 0)
    place = iota((16, RIM), 1) == jnp.where(side < 4, side, jnp.where(side < 8, side + RIM - 8, -1))
    halo[0:8] = jnp.zeros((8, RIM), F32)
    halo[mels : mels + 8] = jnp.zeros((8, RIM), F32)
    halo[4 : mels + 4] = dot(sides, place.astype(BF16), ((0,), (0,)))
    rim = halo[pl.ds(pl.multiple_of(me_m * rows, 8), BAND), :]
    near = jnp.concatenate([jnp.concatenate([above, own, below], axis=0), rim], axis=1)
    x3[...] = jnp.concatenate(
        [
            pltpu.roll(near, 1, 1) * behind,
            near,
            pltpu.roll(near, wide - 1, 1) * ahead,
            jnp.broadcast_to(usable, (BAND, wide)),
            jnp.zeros((128 - 4 * BAND, wide), F32),
        ],
        axis=0,
    ).astype(BF16)
    pre_one[2 * chan : (rows + 4) * chan] = dot(w1[2 * chan : (rows + 4) * chan, :], x3[...])
    lane = iota((1, 128), 1)
    parts = jnp.where(lane < 92, every(SUMS) + every(SUMS + 1) + every(SUMS + 2), 0.0)
    centres, numbers = parts[:, 90:91], parts[:, 91:92]
    centre = jnp.sum(centres * numbers, axis=0, keepdims=True)
    centre = centre / jnp.maximum(jnp.sum(numbers, axis=0, keepdims=True), 1.0)
    delta = centres - centre
    features = jnp.sum(parts + delta * numbers * jnp.where(lane < 81, delta, 1.0), axis=0, keepdims=True)
    moved = jnp.sum(delta * parts, axis=0, keepdims=True)
    def edge_row(k, n):
        first = FIRST * k * count + n
        return jnp.concatenate(
            [got[pl.ds(first, count, stride=FIRST), :], got[pl.ds(first + 8, count, stride=FIRST), :]], axis=1
        )

    edge_rows = [[edge_row(k, n) for n in (0, 1, 6, 7)] for k in range(n_mel)]
    zero = jnp.zeros((count, frame_dev), F32)
    rows_of = [[], [], []]
    for k, (top, second, fore, bottom) in enumerate(edge_rows):
        for n, v in enumerate((edge_rows[k - 1][3] if k else zero, top, second)):
            rows_of[n].append(v)
        for n, v in enumerate((fore, bottom, edge_rows[k + 1][0] if k + 1 < n_mel else zero)):
            rows_of[n].append(v)
    f_usable, f_behind, f_ahead = (all_masks[n * count : (n + 1) * count, :] for n in range(3))
    lane = iota((count, frame_dev), 1)

    def frame_before(v):
        v = pltpu.roll(v, 1, 1)
        return jnp.where(lane == 0, pltpu.roll(v, 1, 0), v) * f_behind

    def frame_after(v):
        v = pltpu.roll(v, frame_dev - 1, 1)
        return jnp.where(lane == frame_dev - 1, pltpu.roll(v, count - 1, 0), v) * f_ahead

    taps = []
    for group in rows_of:
        for move in (frame_before, lambda v: v, frame_after):
            taps.append(jnp.concatenate([move(v) for v in group], axis=1))
    f_usable = jnp.concatenate([f_usable] * (2 * n_mel), axis=1)
    borders = (taps, f_usable)
    edge = strips[...]
    q_usable, q_behind, q_ahead = (edge_masks[:, n : n + 1] for n in range(3))
    lane = iota((count * 8, 128), 1)
    inside = (lane < mels) & (lane % rows != 0) & (lane % rows != rows - 1)
    shifted = [
        pltpu.roll(edge, 1, 0) * q_behind,
        edge,
        pltpu.roll(edge, count * 8 - 1, 0) * q_ahead,
    ]
    taps = [pltpu.roll(v, (1 - i) % 128, 1) if i != 1 else v for i in range(3) for v in shifted]
    features = features + feature_rows(centre, borders, (taps, jnp.where(inside, q_usable, 0.0)))
    features = jnp.where(iota((1, 128), 1) < 90, features, 0.0)
    near_mean = jnp.sum(singles[...] * features, axis=1, keepdims=True) / total
    around = jnp.sum(singles[...], axis=1, keepdims=True)
    square = jnp.sum(pairs[...] * features, axis=1, keepdims=True)
    square = (square + 2.0 * around * jnp.sum(singles[...] * moved, axis=1, keepdims=True)) / total
    inv = lax.rsqrt(square - near_mean * near_mean + 1e-05)
    mean = near_mean + centre * around
    lane = iota((chan, 128), 1)
    stats[0:chan] = jnp.where(lane == 0, mean, jnp.where(lane == 1, inv, 0.0))
    stats[chan : chan + 8] = jnp.broadcast_to(to_lanes(near_mean), (8, 128))
    stats[chan + 8 : chan + 16] = jnp.broadcast_to(to_lanes(inv), (8, 128))
    scale = 0.5 * to_column(params[0:1], chan) * inv
    shift = 0.5 * to_column(params[1:2], chan) - mean * scale
    stats[chan + 16 :] = jnp.where(lane == 0, scale, jnp.where(lane == 1, shift, 0.0))
    scale = jnp.broadcast_to(scale, (chan, wide))
    shift = jnp.broadcast_to(shift, (chan, wide))
    block, taps = wf.shape
    first = jnp.zeros((chan, 128), F32)
    second = jnp.zeros((chan, 128), F32)
    own_mask = usable[:, :frame_dev]
    low_masks = [m.astype(BF16) for m in (usable, behind, ahead)]
    for r in range(2, rows + 4):
        value, _ = silu_halves(pre_one[r * chan : (r + 1) * chan, :] * scale + shift)
        if not 0 <= r - 3 < rows:
            value = value * row_valid(r - 3, rows)
        act_row(act, r, value.astype(BF16), low_masks)
        if r < 5 or r % 2 == 0:
            continue
        g = (r - 3) // 2
        result = dot(wf[...], act[g * 3 * block : g * 3 * block + taps, :frame_dev])
        at = (g - 1) * block
        pre_two[at : at + block, :frame_dev] = result
        if g % 2 == 0:
            beside = [act[n * 3 * block : n * 3 * block + taps, frame_dev:] for n in (g - 1, g)]
            beside = dot(wf[...], jnp.concatenate(beside, axis=1))
            for n in range(2):
                pre_two[at + (n - 1) * block : at + n * block, frame_dev:] = beside[:, n * RIM : (n + 1) * RIM]
        for q in range(2):
            p = result[q * chan : (q + 1) * chan]
            masked = p * own_mask
            first = first + halves(masked)
            second = second + halves(masked * p)
    moved = dot(jnp.broadcast_to(moved, (8, 128)), twice[...], precision=EXACT)[0:1]
    features_out[...] = jnp.concatenate(
        [features + moved, jnp.broadcast_to(centre, (1, 128)), jnp.zeros((6, 128), F32)], axis=0
    )
    share = share_of(devices, chan)

    def put(n, value):
        rows_out[pl.ds(n, devices, stride=SECOND), :] = jnp.broadcast_to(value, (devices, 128))

    for n in range(share):
        put(3 + n, moved_rows(every(EDGES + share + n), count))
        put(3 + share + n, moved_rows(every(EDGES + n), -count))
    for n in [0, 1, 2] + list(range(3 + 2 * share, SECOND - 1)):
        put(n, jnp.zeros((1, 128), F32))
    lane = iota((devices, 128), 1)
    tm = iota((devices, 128), 0) % count
    lefts = jnp.where(lane >= SIDE, every(SUMS), 0.0)
    rights = jnp.where(lane >= SIDE, every(SUMS + 1), 0.0)
    beside = jnp.zeros((devices, 128), F32)
    for n, step in enumerate((0, count, -count)):
        one = jnp.where(tm > 0, moved_rows(rights, step + 1), 0.0)
        two = jnp.where(tm < count - 1, moved_rows(lefts, step - 1), 0.0)
        beside = beside + pltpu.roll(one, (32 * n - SIDE) % 128, 1) + pltpu.roll(two, (32 * n + 16 - SIDE) % 128, 1)
    put(SECOND - 1, beside)
    first = jnp.sum(first, axis=1, keepdims=True)
    second = jnp.sum(second, axis=1, keepdims=True)
    parts = list(three_parts(to_lanes(first) + to_lanes(second, chan)))
    parts = jnp.concatenate(parts + [jnp.zeros((SECOND - 3, 128), F32)], axis=0)
    for d in range(devices):
        payload[d] = (rows_out[SECOND * d : SECOND * (d + 1), :] + parts).astype(BF16)


def spreading(half):
    lane = iota((half, 2 * half), 1)
    return jnp.where(lane >> 1 == iota((half, 2 * half), 0), 0.25, 0.0).astype(BF16)


def half_share(devices, taps):
    return -(-taps // 2 // devices)


def backward_scaled(recv, pre_two, act, own_rows, params, masks,
                    grad, kept_half, sent_half, totals, stats, up, right, got, halved):
    devices = recv.shape[0]
    got[...] = recv[:, 0:SECOND, :].astype(F32).reshape(devices * SECOND, 128)
    chan = params.shape[1]
    half = own_rows.shape[1]
    frame_dev = 2 * half
    rows = MEL_ROWS
    up[...] = dot(own_rows[...], spreading(half))
    usable = masks[0:1, :frame_dev]
    total = masks[3:4, 0:1]
    sums = [got[pl.ds(n, devices, stride=SECOND), :] for n in range(3)]
    sums = jnp.sum(sums[0] + sums[1] + sums[2], axis=0, keepdims=True)
    mean = to_column(sums, chan) / total
    inv = lax.rsqrt(to_column(sums, chan, chan) / total - mean * mean + 1e-05)
    scale = 0.5 * to_column(params[2:3], chan) * inv
    shift = 0.5 * to_column(params[3:4], chan) - mean * scale
    lane = iota((chan, 128), 1)
    columns = jnp.zeros((chan, 128), F32)
    for n, column in enumerate((mean, inv, scale, shift)):
        columns = jnp.where(lane == n, column, columns)
    stats[0:chan] = columns
    stats[chan : chan + 8] = jnp.broadcast_to(to_lanes(inv), (8, 128))
    mean, inv, scale, shift = (jnp.broadcast_to(v, (chan, frame_dev)) for v in (mean, inv, scale, shift))
    first = jnp.zeros((chan, 128), F32)
    second = jnp.zeros((chan, 128), F32)
    mask = 0.5 * usable
    right[3 * chan :] = jnp.ones((16, rows * frame_dev), BF16)
    table = jnp.zeros((9 * chan, 3 * chan + 16), F32)
    for m in range(rows):
        at = slice(m * chan, (m + 1) * chan)
        pre = pre_two[at, :frame_dev]
        _, slope = silu_halves(pre * scale + shift)
        g = up[m // 2 * chan : (m // 2 + 1) * chan, :] * slope * mask
        grad[at, :] = g
        normed = (pre - mean) * inv
        first = first + halves(g * normed)
        second = second + halves(g)
        lanes = slice(m * frame_dev, (m + 1) * frame_dev)
        right[0:chan, lanes] = g.astype(BF16)
        right[chan : 2 * chan, lanes] = normed.astype(BF16)
        right[2 * chan : 3 * chan, lanes] = (g - right[0:chan, lanes].astype(F32)).astype(BF16)
        if m in (5, 11, rows - 1):
            start = m - m % 6
            left = [act[(n + 2) * 3 * chan : (n + 5) * 3 * chan, :frame_dev] for n in range(start, m + 1)]
            lanes = slice(start * frame_dev, (m + 1) * frame_dev)
            table = table + dot(jnp.concatenate(left, axis=1), right[:, lanes], ((1,), (1,)))
    first = jnp.sum(first, axis=1, keepdims=True)
    second = jnp.sum(second, axis=1, keepdims=True)
    totals[...] = jnp.broadcast_to(to_lanes(first) + to_lanes(second, chan), (8, 128))
    rest = jnp.concatenate([table[:, 2 * chan :], jnp.zeros((9 * chan, chan - 16), F32)], axis=1)
    both = table[:, : 2 * chan] + jnp.where(iota(rest.shape, 1) < chan, rest, 0.0)
    single = rest[:, chan : chan + 1]
    taps = 9 * chan // 2
    lane = iota((devices, 128), 1)
    for h in range(2):
        halved[h, 0:taps] = both[h * taps : (h + 1) * taps]
        constants = jnp.zeros((devices, 128), F32)
        for k in range(half_share(devices, 9 * chan)):
            at = h * taps + k * devices
            ones = single[at : min(at + devices, (h + 1) * taps)]
            if ones.shape[0] < devices:
                ones = jnp.concatenate([ones, jnp.zeros((devices - ones.shape[0], 1), F32)], axis=0)
            constants = jnp.where(lane == k, ones, constants)
        halved[h, taps:] = constants
    core = lax.axis_index("tm") % 2
    kept_half[...] = halved[core]
    sent_half[...] = halved[1 - core]


def around(recv, pre_two, act, w1, wf, x3, stats_one, masks, stats, pre_ring, ring, rim, pairs,
           sides, up, got, beyond, more):
    devices = recv.shape[0]
    got[...] = recv[:, 0:SECOND, :].astype(F32).reshape(devices * SECOND, 128)
    rows = MEL_ROWS
    many = rows // 2
    wide = pre_two.shape[1]
    frame_dev = wide - RIM
    chan = pre_two.shape[0] // rows
    usable = masks[0:1]
    low_masks = [masks[n : n + 1].astype(BF16) for n in range(3)]
    scale = jnp.broadcast_to(stats_one[chan + 16 :, 0:1], (chan, wide))
    shift = jnp.broadcast_to(stats_one[chan + 16 :, 1:2], (chan, wide))
    for h, start in enumerate((0, rows + 4)):
        pre_one = dot(w1[start * chan : (start + 2) * chan, :], x3[...])
        for n in range(2):
            value, _ = silu_halves(pre_one[n * chan : (n + 1) * chan] * scale + shift)
            value = value * row_valid(start + n - 3, rows)
            act_row(more, 2 * h + n, value.astype(BF16), low_masks)
    line = 3 * chan
    above = jnp.concatenate([more[0 : 2 * line, :], act[2 * line : 4 * line, :]], axis=0)
    below = jnp.concatenate([act[(rows + 2) * line : (rows + 4) * line, :], more[2 * line :, :]], axis=0)
    pre_ring[0 : 2 * chan] = dot(wf[...], above)
    pre_ring[2 * chan :] = dot(wf[...], below)
    share = share_of(devices, chan)
    holders = chan // share

    def every(n):
        return got[pl.ds(n, devices, stride=SECOND), :]

    beside = every(SECOND - 1)[:holders]
    lane = iota((holders, RIM), 1)
    for n in range(share):
        first = n * holders
        beyond[first : first + holders, :] = every(3 + n)[:holders]
        beyond[chan + first : chan + first + holders, :] = every(3 + share + n)[:holders]
        for r in range(many + 2):
            at = many * n + (r if r < many else 32 + many - 1 if r == many else 64)
            left, right_of = beside[:, at : at + 1], beside[:, at + 16 : at + 17]
            side = jnp.where(lane >= RIM - 2, 0.25 * left, jnp.where(lane < 2, 0.25 * right_of, 0.0))
            sides[r * chan + first : r * chan + first + holders, :] = side
    up[...] = dot(beyond[...].astype(BF16), spreading(frame_dev // 2))
    scale = jnp.broadcast_to(stats[0:chan, 2:3], (chan, wide))
    shift = jnp.broadcast_to(stats[0:chan, 3:4], (chan, wide))
    for n, m in enumerate((-2, -1, rows, rows + 1)):
        below = n // 2
        upstream = jnp.concatenate(
            [
                up[below * chan : (below + 1) * chan, :],
                sides[(many + below) * chan : (many + below + 1) * chan, :],
            ],
            axis=1,
        )
        _, slope = silu_halves(pre_ring[n * chan : (n + 1) * chan, :] * scale + shift)
        ring[n * chan : (n + 1) * chan, :] = upstream * slope * (usable * (0.5 * row_valid(m, rows)))
    both = None
    for m in range(rows):
        at = slice(m * chan, (m + 1) * chan)
        _, slope = silu_halves(pre_two[at, frame_dev:] * scale[:, frame_dev:] + shift[:, frame_dev:])
        upstream = sides[m // 2 * chan : (m // 2 + 1) * chan, :]
        rim[m * chan : (m + 1) * chan, :] = upstream * slope * (0.5 * usable[:, frame_dev:])
        value, _ = silu_halves(pre_two[at, :frame_dev] * scale[:, :frame_dev] + shift[:, :frame_dev])
        value = value * usable[:, :frame_dev]
        both = value if m % 2 == 0 else both + value
        if m % 2:
            pairs[m // 2 * chan : (m // 2 + 1) * chan, :] = both


def pack_sums(kept_half, received, totals, after, payload):
    del after
    devices = kept_half.shape[0] - TAPS // 2
    block = payload.shape[0] // devices
    payload[pl.ds(0, devices, stride=block), :] = jnp.broadcast_to(totals[0:1], (devices, 128))
    taps = TAPS // 2
    total = kept_half[...] + received[...]
    for k in range(block - 2):
        cut = total[k * devices : min((k + 1) * devices, taps)]
        if cut.shape[0] < devices:
            cut = jnp.concatenate([cut, jnp.zeros((devices - cut.shape[0], 128), F32)], axis=0)
        payload[pl.ds(1 + k, devices, stride=block), :] = cut
    payload[pl.ds(block - 1, devices, stride=block), :] = total[taps:]


def pool(totals, pairs, out, gain_out, bias_out, temp):
    gain_out[...] = totals[0:1, : gain_out.shape[1]]
    bias_out[...] = totals[0:1, gain_out.shape[1] :]
    chan, rows, half = out.shape[1:]
    to_mean = jnp.where(iota((2 * half, half), 0) >> 1 == iota((2 * half, half), 1), 0.25, 0.0)
    pooled = dot(pairs[...], to_mean, precision=EXACT)
    for r in range(rows):
        temp[pl.ds(r, chan, stride=rows), :] = pooled[r * chan : (r + 1) * chan]
    out[0] = temp[...].reshape(chan, rows, half).astype(BF16)


def backward(recv, pre_two, pre_ring, grad, ring, rim, stats_two, w1, x3, stats, params, masks, wb,
             out, own_low, payload, totals, g3, pre_one, g1):
    chan = params.shape[1]
    rows = MEL_ROWS
    wide = pre_two.shape[1]
    frame_dev = wide - RIM
    usable = masks[0:1]
    behind, ahead = (masks[n : n + 1].astype(BF16) for n in (1, 2))
    total = masks[3:4, 0:1]
    devices = payload.shape[0] // 14
    pre_one[...] = dot(w1[3 * chan : (rows + 3) * chan], x3[:, :frame_dev])

    even, odd = summed_blocks(recv, devices, 2)
    sums = even[0:1] + odd[0:1]
    gain_sum, bias_sum = sums[:, :chan], sums[:, chan:]
    totals[...] = jnp.broadcast_to(sums, (8, 128))
    mean, inv = stats_two[0:chan, 0:1], stats_two[0:chan, 1:2]
    factor = to_column(params[2:3], chan) * inv
    gain_part = factor * (to_column(sums, chan) / total * inv)
    bias_part = factor * (to_column(sums, chan, chan) / total) - mean * gain_part
    gain_part = jnp.broadcast_to(gain_part, (chan, wide))
    bias_part = jnp.broadcast_to(bias_part, (chan, wide))
    factor = jnp.broadcast_to(factor, (chan, wide))
    scale = jnp.broadcast_to(stats[chan + 16 :, 0:1], (chan, frame_dev))
    shift = jnp.broadcast_to(stats[chan + 16 :, 1:2], (chan, frame_dev))
    factor_one = jnp.broadcast_to(to_column(params[0:1], chan) * stats[0:chan, 1:2], (chan, frame_dev))
    own_mask = 0.5 * usable[:, :frame_dev]
    count = rows + 4
    share = even.shape[0] - 2
    mine = jnp.concatenate([even[1 : share + 1], odd[1 : share + 1]], axis=0)
    single = jnp.concatenate([to_column(v[share + 1 :], share) for v in (even, odd)], axis=0)
    factor_l = params[2:3] * stats_two[chan : chan + 1, :chan]
    mine = mine[:, :chan] - (bias_sum * single + gain_sum * mine[:, chan:]) / total
    mine = factor_l * mine
    mine = jnp.concatenate([mine[:share], mine[share:]], axis=1)
    if share < 9:
        mine = jnp.concatenate([mine, jnp.zeros((9 - share, 128), F32)], axis=0)
    table = jnp.zeros((chan, 128), F32)

    def tap_sums(m):
        part = g1[m * chan : (m + 4) * chan, :]
        high = lax.reduce_precision(part, 8, 7)
        low = (part - high).astype(BF16)
        taps_in = x3[:, :frame_dev]
        products = dot(high.astype(BF16), taps_in, ((1,), (1,))) + dot(low, taps_in, ((1,), (1,)))
        moved = [pltpu.roll(products[k * chan : (k + 1) * chan], 128 - (m + k + 3), 1) for k in range(4)]
        return (moved[0] + moved[1]) + (moved[2] + moved[3])

    for q in range(count):
        at = slice(q * chan, (q + 1) * chan)
        mask = usable if 0 <= q - 2 < rows else usable * row_valid(q - 2, rows)
        if 2 <= q < rows + 2:
            own = slice((q - 2) * chan, (q - 1) * chan)
            pre, scaled = pre_two[own, :], jnp.concatenate([grad[own, :], rim[own, :]], axis=1)
        else:
            n = q if q < 2 else q - rows
            pre, scaled = pre_ring[n * chan : (n + 1) * chan, :], ring[n * chan : (n + 1) * chan, :]
        low = (factor * scaled - (bias_part + pre * gain_part) * mask).astype(BF16)
        out[at, :] = low
        if not 1 <= q < count - 1:
            continue
        base = (q - 1) * 3 * chan
        for n, v in enumerate((low,) + shifted_frames(low, behind, ahead)):
            spot = base + (1, 0, 2)[n] * chan
            g3[spot : spot + chan, :] = v[:, :frame_dev]
        start = q - 4
        if start < 0 or start % 2:
            continue
        result = dot(wb[...], g3[start * 3 * chan : (start + 4) * 3 * chan, :])
        for n in range(2):
            m = start + n
            at = slice(m * chan, (m + 1) * chan)
            _, slope = silu_halves(pre_one[at, :] * scale + shift)
            value = result[n * chan : (n + 1) * chan] * slope * own_mask
            own_low[at, :] = (value * factor_one).astype(BF16)
            g1[at, :] = value
        if start % 4 == 2 and start > 2:
            table = table + tap_sums(start - 6)
    table = table + tap_sums(rows - 4)
    table = table.T
    places = [BAND * j + i for i in range(3) for j in range(3)] + [3 * BAND]
    rows10 = jnp.concatenate([table[n : n + 1] for n in places], axis=0)
    sums = jnp.concatenate([rows10[0:5], rows10[5:10]], axis=1)
    block = jnp.concatenate([sums, mine], axis=0)
    block = jnp.concatenate([block] * 4, axis=0)
    for d in range(0, devices, 4):
        payload[14 * d : 14 * (d + 4), :] = block


def transposed(grad, own_low, w1, wb, x3, stats, features, k1t, params, masks, ws_hbm,
               first, ws, normed_taps, low, g3, rim, sem):
    load = pltpu.make_async_copy(ws_hbm, ws, sem)
    load.start()
    rows = MEL_ROWS
    chan = own_low.shape[0] // rows
    wide = grad.shape[1]
    frame_dev = wide - RIM
    count = grad.shape[0] // chan
    usable = masks[0:1]
    behind, ahead = (masks[n : n + 1].astype(BF16) for n in (1, 2))
    scale = jnp.broadcast_to(stats[chan + 16 :, 0:1], (chan, wide))
    shift = jnp.broadcast_to(stats[chan + 16 :, 1:2], (chan, wide))
    factor = jnp.broadcast_to(to_column(params[0:1], chan) * stats[0:chan, 1:2], (chan, wide))
    edge = (0, 1, 2, 3, count - 4, count - 3, count - 2, count - 1)
    for q in range(count):
        value = grad[q * chan : (q + 1) * chan, :]
        for n, v in enumerate((value,) + shifted_frames(value, behind, ahead)):
            spot = (3 * q + (1, 0, 2)[n]) * chan
            rim[spot : spot + chan, :] = v[:, frame_dev:]
            if q in edge:
                spot = (3 * edge.index(q) + (1, 0, 2)[n]) * chan
                g3[spot : spot + chan, :] = v[:, :frame_dev]
    low[chan : (rows + 1) * chan, :frame_dev] = own_low[...]

    def put(m, lanes, result, pre_one):
        at = slice((m + 1) * chan, (m + 2) * chan)
        _, slope = silu_halves(pre_one * scale[:, lanes] + shift[:, lanes])
        mask = usable[:, lanes] * (0.5 * row_valid(m, rows))
        low[at, lanes] = (result * slope * mask * factor[:, lanes]).astype(BF16)

    pre_one = dot(w1[2 * chan : (rows + 4) * chan, :], x3[:, frame_dev:])
    beside = slice(frame_dev, wide)
    for start in range(0, rows + 2, 2):
        result = dot(wb[...], rim[start * 3 * chan : (start + 4) * 3 * chan, :])
        for n in range(2):
            at = slice((start + n) * chan, (start + n + 1) * chan)
            put(start + n - 1, beside, result[n * chan : (n + 1) * chan], pre_one[at])
    own = slice(0, frame_dev)
    result = dot(wb[...], g3[: 4 * 3 * chan, :])
    put(-1, own, result[:chan], dot(w1[2 * chan : 3 * chan, :], x3[:, :frame_dev]))
    result = dot(wb[...], g3[4 * 3 * chan :, :])
    put(rows, own, result[chan:], dot(w1[(rows + 3) * chan : (rows + 4) * chan, :], x3[:, :frame_dev]))
    row = features[0:1, :]
    lane = iota((1, 128), 1)
    gram = jnp.concatenate(
        [jnp.where(lane < 9, pltpu.roll(row, 128 - 9 * t, 1) if t else row, 0.0) for t in range(9)]
        + [jnp.zeros((7, 128), F32)],
        axis=0,
    )
    single = to_column(row, 16, 81)[0:9]
    k_rows = jnp.concatenate([k1t[...], jnp.zeros((112, chan), F32)], axis=0)
    mean_l, inv_l = stats[chan : chan + 1, :chan], stats[chan + 8 : chan + 9, :chan]
    normed = inv_l * (dot(gram, k_rows, precision=EXACT)[0:9] - single * mean_l)
    normed_taps[0:16] = jnp.concatenate([normed, jnp.zeros((7, chan), F32)], axis=0)
    normed_taps[16:32] = jnp.broadcast_to(to_column(row, 16, 81), (16, chan))
    load.wait()
    first[...] = dot(ws[...], low[...])


def finish(recv, features, stats, k1t, first, ws, w1, x3, normed_taps, params, masks,
           spec_hbm, kernel_one_hbm, kernel_two_hbm, gain_hbm, bias_hbm,
           spec_grad, kernel_one, kernel_two, gain_out, bias_out, sems):
    chan = params.shape[1]
    rows = MEL_ROWS
    wide = x3.shape[1]
    frame_dev = wide - RIM
    usable, behind, ahead = (masks[n : n + 1] for n in range(3))
    total = masks[3:4, 0:1]
    gain = params[0:1]
    count = recv.shape[0] // 14
    share = half_share(count, 9 * chan)
    sums = summed_blocks(recv, count)[0:5]
    ten = jnp.concatenate([sums[:, :chan], sums[:, chan:]], axis=0)
    bias_sum = ten[9:10]
    mean_l, inv_l = stats[chan : chan + 1, :chan], stats[chan + 8 : chan + 9, :chan]
    ten = ten - features[1:2, 0:1] * bias_sum
    k = k1t[0:9]
    gain_sum = inv_l * (jnp.sum(k * ten[0:9], axis=0, keepdims=True) - mean_l * bias_sum)
    gain_out[...] = gain_sum
    bias_out[...] = bias_sum
    factor_l = gain * inv_l
    scale = factor_l * gain_sum / total * inv_l
    scale = jnp.concatenate(
        [scale * row_valid(-1, rows)] + [scale] * rows + [scale * row_valid(rows, rows)], axis=1
    )
    many = 3 * rows

    def in_parts(v, right):
        high = lax.reduce_precision(v, 8, 7)
        v = dot(jnp.concatenate([high, v - high], axis=0).astype(BF16), right)
        return v[:many] + v[many:]

    combined = in_parts(ws[...].astype(F32) * scale, w1[2 * chan : (rows + 4) * chan, :])
    left = [recv[pl.ds(5 + p, count, stride=14), :] for p in range(share)]
    taps = TAPS // 2
    whole = [jnp.concatenate([v[:, h * chan : (h + 1) * chan] for v in left], axis=0)[:taps] for h in range(2)]
    whole = jnp.concatenate(whole, axis=0)
    for t in range(9):
        kernel_two[t] = whole[t * chan : (t + 1) * chan].T
    stores = [pltpu.make_async_copy(kernel_two, kernel_two_hbm, sems.at[4])]
    stores[0].start()
    taken = in_parts(combined, x3[...])
    taps = first[...] - taken
    moved = [taps[rows * b : rows * (b + 1)] for b in range(3)]
    mean_full = mean_l + features[1:2, 0:1] * jnp.sum(k, axis=0, keepdims=True)
    constant = jnp.sum(k * (factor_l * (bias_sum - gain_sum * inv_l * mean_full) / total), axis=1, keepdims=True)
    for a in range(3):
        row = iota((rows, 1), 0) + (a - 1) + lax.axis_index("mel") * rows
        valid = ((row >= 0) & (row < lax.axis_size("mel") * rows)).astype(F32) * usable
        for b in range(3):
            t = 3 * (2 - a) + 2 - b
            moved[b] = moved[b] - constant[t : t + 1] * valid
    result = pltpu.roll(moved[0], 1, 1) * behind + moved[1] + pltpu.roll(moved[2], wide - 1, 1) * ahead
    spec_grad[0] = (result * usable)[:, :frame_dev]
    grad_taps = factor_l * (ten[0:9] - (bias_sum * normed_taps[16:25] + gain_sum * normed_taps[0:9]) / total)
    for i in range(3):
        kernel_one[i] = grad_taps[3 * i : 3 * i + 3]
    outs = ((spec_grad, spec_hbm), (kernel_one, kernel_one_hbm), (gain_out, gain_hbm), (bias_out, bias_hbm))
    wait_all(stores + start_all(*outs, sems=sems))


def run(kernel, outs, scratch, *args, hbm=0, apart=(), flops=10**8, size=4 * 10**6):
    vmem = pl.BlockSpec(memory_space=pltpu.VMEM)
    devices = lax.axis_size("mel") * lax.axis_size("tm")
    specs = []
    args = list(args)
    for n, a in enumerate(args):
        if hbm and n >= len(args) - hbm:
            specs.append(pl.BlockSpec(memory_space=pltpu.HBM))
            args[n] = pltpu.with_memory_space_constraint(a, pltpu.HBM)
        else:
            specs.append(vmem)
            args[n] = pltpu.with_memory_space_constraint(a, pltpu.VMEM)
    return pl.pallas_call(
        kernel,
        out_shape=outs,
        in_specs=specs,
        out_specs=[pl.BlockSpec(memory_space=pltpu.HBM) if n in apart else vmem for n in range(len(outs))],
        scratch_shapes=scratch,
        compiler_params=pltpu.CompilerParams(vmem_limit_bytes=(29 + devices // 32) * 2**20),
        cost_estimate=pl.CostEstimate(flops=flops, bytes_accessed=size, transcendentals=0),
    )(*args)


def shape(dims, dtype=F32):
    return jax.ShapeDtypeStruct(dims, dtype)


def kept(dims, dtype=F32):
    return pltpu.VMEM(dims, dtype)


def far(dims, dtype=F32):
    return pltpu.HBM(dims, dtype)


def exchange(blocks, axes=AXES):
    return lax.all_to_all(blocks, axes, 0, 0, tiled=True)


def exchange_rows(rows, axes=AXES):
    return exchange(rows[:, None, :], axes)[:, 0, :]


def shards(spectrum, clip_bounds, kernel_one, gain_one, bias_one, kernel_two, gain_two, bias_two, pooled_grad):
    _, rows, frame_dev = spectrum.shape
    chan = kernel_two.shape[0]
    n_mel, n_tm = lax.axis_size("mel"), lax.axis_size("tm")
    devices = n_mel * n_tm
    half = frame_dev // 2
    wide = frame_dev + RIM
    mels = n_mel * rows

    packed, own, spec, masks = run(
        pack,
        [
            kept((devices, FIRST, 128), BF16),
            kept(pooled_grad.shape, BF16),
            kept(spectrum.shape, BF16),
            kept((8, wide)),
        ],
        [
            pltpu.SMEM(clip_bounds.shape, jnp.int32),
            pltpu.VMEM((2 * chan, half), F32),
            pltpu.VMEM((devices * FIRST, 128), F32),
            pltpu.SemaphoreType.DMA((3,)),
        ],
        spectrum,
        pooled_grad,
        clip_bounds,
        hbm=3,
    )
    recv = exchange(packed)
    ext = rows + 6
    span = 4 * 3 * chan
    wf, wb, w1, ws, pairs, singles, k1t, params, all_masks, edge_masks, twice, own_rows = run(
        weights,
        [
            kept((2 * chan, span), BF16),
            kept((2 * chan, span), BF16),
            kept((ext * chan, 128), BF16),
            far((rows * 3, (rows + 2) * chan), BF16),
            kept((chan, 128)),
            kept((chan, 128)),
            kept((16, chan)),
            kept((8, chan)),
            kept((3 * n_tm, frame_dev)),
            kept((n_tm * 8, 128)),
            kept((128, 128)),
            kept((chan * rows // 2, half), BF16),
        ],
        [
            pltpu.VMEM((9, chan, chan), BF16),
            pltpu.VMEM((3, 3, chan), BF16),
            pltpu.VMEM((4, 1, chan), F32),
            pltpu.SMEM(clip_bounds.shape, jnp.int32),
            pltpu.VMEM((rows * 3, (rows + 2) * chan), BF16),
            pltpu.VMEM((chan * rows // 2, half), F32),
            pltpu.SemaphoreType.DMA((8,)),
        ],
        own,
        clip_bounds,
        jnp.transpose(kernel_two, (2, 3, 0, 1)).reshape(9, chan, chan),
        jnp.transpose(kernel_one, (1, 2, 0)),
        gain_one[None],
        bias_one[None],
        gain_two[None],
        bias_two[None],
        hbm=7,
        apart=(3,),
    )
    pre_two, payload, act, x3, stats_one, features = run(
        forward_one,
        [
            kept((rows * chan, wide)),
            kept((devices, SECOND, 128), BF16),
            kept((ext * 3 * chan, wide), BF16),
            kept((128, wide), BF16),
            kept((2 * chan + 16, 128)),
            kept((8, 128)),
        ],
        [
            pltpu.VMEM((ext * chan, wide), F32),
            pltpu.VMEM((devices * FIRST, 128), F32),
            pltpu.VMEM((n_tm * 8, 128), F32),
            pltpu.VMEM((mels + 8, RIM), F32),
            pltpu.VMEM((devices * SECOND, 128), F32),
        ],
        recv,
        spec,
        pairs,
        singles,
        twice,
        w1,
        wf,
        params,
        masks,
        all_masks,
        edge_masks,
    )
    recv = exchange(payload)
    grad, kept_half, sent_half, totals, stats_two = run(
        backward_scaled,
        [
            kept((rows * chan, frame_dev)),
            kept((TAPS // 2 + devices, 128)),
            kept((TAPS // 2 + devices, 128)),
            kept((8, 128)),
            kept((chan + 8, 128)),
        ],
        [
            pltpu.VMEM((rows // 2 * chan, frame_dev), F32),
            pltpu.VMEM((3 * chan + 16, rows * frame_dev), BF16),
            pltpu.VMEM((devices * SECOND, 128), F32),
            pltpu.VMEM((2, TAPS // 2 + devices, 128), F32),
        ],
        recv,
        pre_two,
        act,
        own_rows,
        params,
        masks,
    )
    received = lax.ppermute(sent_half, "tm", [(i, i ^ 1) for i in range(n_tm)])
    pre_ring, ring, rim, row_pairs = run(
        around,
        [kept((4 * chan, wide)), kept((4 * chan, wide)), kept((rows * chan, RIM)), kept((rows // 2 * chan, frame_dev))],
        [
            pltpu.VMEM(((rows // 2 + 2) * chan, RIM), F32),
            pltpu.VMEM((2 * chan, frame_dev), F32),
            pltpu.VMEM((devices * SECOND, 128), F32),
            pltpu.VMEM((2 * chan, half), F32),
            pltpu.VMEM((4 * 3 * chan, wide), BF16),
        ],
        recv,
        pre_two,
        act,
        w1,
        wf,
        x3,
        stats_one,
        masks,
        stats_two,
    )
    (payload,) = run(
        pack_sums,
        [kept((devices * (half_share(devices, 9 * chan) + 2), 128))],
        [],
        kept_half,
        received,
        totals,
        rim,
    )
    recv = exchange_rows(payload)
    grad, own_low, payload, totals = run(
        backward,
        [
            kept(((rows + 4) * chan, wide), BF16),
            kept((rows * chan, frame_dev), BF16),
            kept((devices * 14, 128)),
            kept((8, 128)),
        ],
        [
            pltpu.VMEM(((rows + 2) * 3 * chan, frame_dev), BF16),
            pltpu.VMEM((rows * chan, frame_dev), F32),
            pltpu.VMEM((rows * chan, frame_dev), F32),
        ],
        recv,
        pre_two,
        pre_ring,
        grad,
        ring,
        rim,
        stats_two,
        w1,
        x3,
        stats_one,
        params,
        masks,
        wb,
    )
    recv = exchange_rows(payload)
    pooled, gain_two_grad, bias_two_grad = run(
        pool,
        [shape((1, chan, rows // 2, half), BF16), shape((1, chan)), shape((1, chan))],
        [
            pltpu.VMEM((rows // 2 * chan, 128), F32),
        ],
        totals,
        row_pairs,
    )
    first, ws, normed_taps = run(
        transposed,
        [
            kept((rows * 3, wide)),
            kept((rows * 3, (rows + 2) * chan), BF16),
            kept((32, chan)),
        ],
        [
            pltpu.VMEM(((rows + 2) * chan, wide), BF16),
            pltpu.VMEM((8 * 3 * chan, frame_dev), BF16),
            pltpu.VMEM(((rows + 4) * 3 * chan, RIM), BF16),
            pltpu.SemaphoreType.DMA,
        ],
        grad,
        own_low,
        w1,
        wb,
        x3,
        stats_one,
        features,
        k1t,
        params,
        masks,
        ws,
        hbm=1,
    )
    spec_grad, kernel_one_grad, kernel_two_grad, gain_one_grad, bias_one_grad = run(
        finish,
        [
            shape((1, rows, frame_dev)),
            shape((3, 3, chan)),
            shape((9, chan, chan)),
            shape((1, chan)),
            shape((1, chan)),
        ],
        [
            pltpu.VMEM((1, rows, frame_dev), F32),
            pltpu.VMEM((3, 3, chan), F32),
            pltpu.VMEM((9, chan, chan), F32),
            pltpu.VMEM((1, chan), F32),
            pltpu.VMEM((1, chan), F32),
            pltpu.SemaphoreType.DMA((5,)),
        ],
        recv,
        features,
        stats_one,
        k1t,
        first,
        ws,
        w1,
        x3,
        normed_taps,
        params,
        masks,
        apart=range(5),
    )
    kernel_two_grad = jnp.transpose(kernel_two_grad.reshape(3, 3, chan, chan), (2, 3, 0, 1))
    return (
        pooled,
        spec_grad,
        jnp.transpose(kernel_one_grad, (2, 0, 1)),
        gain_one_grad[0],
        bias_one_grad[0],
        kernel_two_grad,
        gain_two_grad[0],
        bias_two_grad[0],
    )


def solution(mesh):
    return jax.shard_map(
        shards,
        mesh=mesh,
        in_specs=(
            P(None, "mel", "tm"),
            P(),
            P(),
            P(),
            P(),
            P(),
            P(),
            P(),
            P(None, None, "mel", "tm"),
        ),
        out_specs=(P(None, None, "mel", "tm"), P(None, "mel", "tm"), P(), P(), P(), P(), P(), P()),
        check_vma=False,
    )
```

profile of v0, /device:TPU:1, one launch (start us, length us, event | category | flops | bytes accessed | tf_op | source)
XLA Modules:
  0.0 61.8 jit_solution(14811417894850897522)
XLA Ops:
  0.6 2.0 %shard_map.152 = (bf16[32,24,128]{2,1,0:T(8,128)(2,1)}, bf16[1,64,8,128]{3,2,1,0:T(8,128)(2,1)S(1)}, bf16[1,16,256]{2,1,0:T(8,128)(2,1)S(1)}, f32[8,384]{1,0:T(8,128)S(1)}) custom-call(bf16[1,16,256]{2,1,0:T(8,128)(2,1)} %spec_hbm.1, bf16[1,64,8,128]{3,2,1,0:T(8,128)(2,1)} %grad_hbm.1, s32[1,4]{1,0:T(1,128)} %bounds_hbm.3), custom_call_target="tpu_custom_call" | custom-call | flops 100000000 | bytes 4000000 | tf_op jit(solution)/shard_map/pallas_call | solution.py:895
  2.7 7.1 %all-to-all-start = ((bf16[32,24,128]{2,1,0:T(8,128)(2,1)}), bf16[32,24,128]{2,1,0:T(8,128)(2,1)S(1)}, u32[]{:S(2)}, u32[]{:S(2)}) async-start(bf16[32,24,128]{2,1,0:T(8,128)(2,1)} %get-tuple-element.54), calls=%async_computation | async-start | bytes 393216 | tf_op jit(solution)/shard_map/all_to_all | solution.py:919
  9.8 2.1 %shard_map.153 = (bf16[128,768]{1,0:T(8,128)(2,1)S(1)}, bf16[128,768]{1,0:T(8,128)(2,1)S(1)}, bf16[1408,128]{1,0:T(8,128)(2,1)S(1)}, bf16[48,1152]{1,0:T(8,128)(...) custom-call(bf16[1,64,8,128]{3,2,1,0:T(8,128)(2,1)S(1)} %get-tuple-e, ...), custom_call_target="tpu_custom_call" | custom-call | flops 100000000 | bytes 4000000 | tf_op jit(solution)/shard_map/pallas_call | solution.py:895
  11.9 7.2 %all-to-all-done.recv = bf16[32,24,128]{2,1,0:T(8,128)(2,1)S(1)} async-done(((bf16[32,24,128]{2,1,0:T(8,128)(2,1)}), bf16[32,24,128]{2,1,0:T(8,128)(2,1)S(1)}, u32[]{:S(2)}, u32[]{:S(2)}) %all-to-all-start) | async-done | bytes 196640 | tf_op jit(solution)/shard_map/all_to_all | solution.py:919
  19.1 2.4 %shard_map.154 = (f32[1024,384]{1,0:T(8,128)S(1)}, bf16[32,8,128]{2,1,0:T(8,128)(2,1)S(1)}, bf16[4224,384]{1,0:T(8,128)(2,1)S(1)}, bf16[128,384]{1,0:T(8,128)(2,...) custom-call(bf16[32,24,128]{2,1,0:T(8,128)(2,1)S(1)} %all-to-all-done.recv, ...), custom_call_target="tpu_custom_call" | custom-call | flops 100000000 | bytes 4000000 | tf_op jit(solution)/shard_map/pallas_call | solution.py:895
  21.5 9.2 %all_to_all.20.recv = bf16[32,8,128]{2,1,0:T(8,128)(2,1)S(1)} all-to-all(bf16[32,8,128]{2,1,0:T(8,128)(2,1)S(1)} %get-tuple-element.66), channel_id=1, replica_groups=mesh['mel'=4,'tm'=8] {'mel','tm'}, dimensions={0} | all-to-all | bytes 131072 | tf_op jit(solution)/shard_map/all_to_all | solution.py:919
  30.7 2.3 %shard_map.155 = (f32[1024,256]{1,0:T(8,128)S(1)}, f32[320,128]{1,0:T(8,128)S(1)}, f32[320,128]{1,0:T(8,128)S(1)}, f32[8,128]{1,0:T(8,128)S(1)}, f32[72,128]{1,0:T(8,128)S(1)}) custom-call(bf16[32,8,128]{2,1,0:T(8,128)(2,1)S(1)} %all_to_all.20.recv, f32[1024,384]{1,0:T(8,128)S(1)} %get-tuple-element.67.pre_two, bf16[4224,384]{1,0:T(8,128)(2,1)S(1)} %get-tuple-element.68.act, ...), custom_call_target="tpu_custom_call" | custom-call | flops 100000000 | bytes 4000000 | tf_op jit(solution)/shard_map/pallas_call | solution.py:895
  33.0 0.4 collective-permute-start
  33.4 1.2 %shard_map.156 = (f32[256,384]{1,0:T(8,128)S(1)}, f32[256,384]{1,0:T(8,128)S(1)}, f32[1024,128]{1,0:T(8,128)S(1)}, f32[512,256]{1,0:T(8,128)S(1)}) custom-call(bf16[32,8,128]{2,1,0:T(8,128)(2,1)S(1)} %all_to_all.20.recv, f32[1024,384]{1,0:T(8,128)S(1)} %get-tuple-element.67.pre_two, bf16[4224,384]{1,0:T(8,128)(2,1)S(1)} %get-tuple-element.68.act, ...), custom_call_target="tpu_custom_call" | custom-call | flops 100000000 | bytes 4000000 | tf_op jit(solution)/shard_map/pallas_call | solution.py:895
  34.6 0.0 collective-permute-done.received
  34.7 10.7 %all_to_all.21 = f32[352,1,128]{2,1,0:T(1,128)S(1)} all-to-all(f32[352,1,128]{2,1,0:T(1,128)S(1)} %bitcast.26), channel_id=1, replica_groups=mesh['mel'=4,'tm'=8] {'mel','tm'}, dimensions={0} | all-to-all | bytes 360448 | tf_op jit(solution)/shard_map/all_to_all | solution.py:919
  45.3 3.1 %shard_map.158 = (bf16[1280,384]{1,0:T(8,128)(2,1)S(1)}, bf16[1024,256]{1,0:T(8,128)(2,1)S(1)}, f32[448,128]{1,0:T(8,128)}, f32[8,128]{1,0:T(8,128)S(1)}) custom-call(f32[352,128]{1,0:T(8,128)S(1)} %bitcast.25, f32[1024,384]{1,0:T(8,128)S(1)} %get-tuple-element.67.pre_two, f32[256,384]{1,0:T(8,128)S(1)} %get-tuple-element.77.pre_ring, ...), custom_call_target="tpu_custom_call" | custom-call | flops 100000000 | bytes 4000000 | tf_op jit(solution)/shard_map/pallas_call | solution.py:895
  48.4 2.3 %all-to-all-start.3 = ((f32[448,1,128]{2,1,0:T(1,128)}), f32[448,1,128]{2,1,0:T(1,128)S(1)}, u32[]{:S(2)}, u32[]{:S(2)}) async-start(f32[448,1,128]{2,1,0:T(1,128)} %bitcast.11), calls=%async_computation.3 | async-start | bytes 458752 | tf_op jit(solution)/shard_map/all_to_all | solution.py:919
  50.7 1.3 %shard_map.159 = (bf16[1,64,8,128]{3,2,1,0:T(8,128)(2,1)}, f32[1,64]{1,0:T(1,128)}, f32[1,64]{1,0:T(1,128)}) custom-call(f32[8,128]{1,0:T(8,128)S(1)} %get-tuple-element.81.totals, f32[512,256]{1,0:T(8,128)S(1)} %get-tuple-element.82.pairs), custom_call_target="tpu_custom_call" | custom-call | flops 100000000 | bytes 4000000 | tf_op jit(solution)/shard_map/pallas_call | solution.py:895
  52.0 2.2 %shard_map.160 = (f32[48,384]{1,0:T(8,128)S(1)}, bf16[48,1152]{1,0:T(8,128)(2,1)S(1)}, f32[32,64]{1,0:T(8,128)S(1)}) custom-call(bf16[1280,384]{1,0:T(8,128)(2,1)S(1)} %get-tuple-element.87.grad, bf16[1024,256]{1,0:T(8,128)(2,1)S(1)} %get-tuple-element.88.own_low, bf16[1408,128]{1,0:T(8,128)(2,1)S(1)} %get-tuple-element.60.w1, ...), custom_call_target="tpu_custom_call" | custom-call | flops 100000000 | bytes 4000000 | tf_op jit(solution)/shard_map/pallas_call | solution.py:895
  54.2 6.2 %all-to-all-done.3 = f32[448,1,128]{2,1,0:T(1,128)S(1)} async-done(((f32[448,1,128]{2,1,0:T(1,128)}), f32[448,1,128]{2,1,0:T(1,128)S(1)}, u32[]{:S(2)}, u32[]{:S(2)}) %all-to-all-start.3) | async-done | bytes 229408 | tf_op jit(solution)/shard_map/all_to_all | solution.py:919
  60.4 1.4 %shard_map.161 = (f32[1,16,256]{2,1,0:T(8,128)}, f32[3,3,64]{2,1,0:T(4,128)}, f32[9,64,64]{2,1,0:T(8,128)}, f32[1,64]{1,0:T(1,128)}, f32[1,64]{1,0:T(1,128)}) custom-call(f32[448,128]{1,0:T(8,128)S(1)} %bitcast.24, f32[8,128]{1,0:T(8,128)S(1)} %get-tuple-element.85.features, f32[144,128]{1,0:T(8,128)S(1)} %get-tuple-element.74.stats_one.stats, ...), custom_call_target="tpu_custom_call" | custom-call | flops 100000000 | bytes 4000000 | tf_op jit(solution)/shard_map/pallas_call | solution.py:895
  (1 shorter events, 0.0 us)
Async XLA Ops:
  2.7 16.4 %all-to-all-start = ((bf16[32,24,128]{2,1,0:T(8,128)(2,1)}), bf16[32,24,128]{2,1,0:T(8,128)(2,1)S(1)}, u32[]{:S(2)}, u32[]{:S(2)}) async-start(bf16[32,24,128]{2,1,0:T(8,128)(2,1)} %get-tuple-element.54), calls=%async_computation | async-start | bytes 393216 | tf_op jit(solution)/shard_map/all_to_all | solution.py:919
  33.0 1.6 %collective-permute-start = (f32[320,128]{1,0:T(8,128)S(1)}, f32[320,128]{1,0:T(8,128)S(1)}, u32[]{:S(2)}, u32[]{:S(2)}) collective-permute-start(f32[320,128]{1,0:T(8,128)S(1)} %get-tuple-element.71), channel_id=1, source_target_pairs={{0,1},{1,0},{2,3},{3,2},{4,5},{5,4},{6,7},{7,6},{8,9},{9,8},{10,11... | collective-permute-start | bytes 491528 | tf_op jit(solution)/shard_map/ppermute | solution.py:1045
  48.4 12.0 %all-to-all-start.3 = ((f32[448,1,128]{2,1,0:T(1,128)}), f32[448,1,128]{2,1,0:T(1,128)S(1)}, u32[]{:S(2)}, u32[]{:S(2)}) async-start(f32[448,1,128]{2,1,0:T(1,128)} %bitcast.11), calls=%async_computation.3 | async-start | bytes 458752 | tf_op jit(solution)/shard_map/all_to_all | solution.py:919
where the time goes:
time: 62.2 us; the launch traced here: 61.8 us
  blocking collectives  19.9 us (32%)
  Pallas kernels  17.9 us (29%)
  waiting for transfers between devices  13.4 us (22%)
  starting transfers between devices  9.88 us (16%)
  between operations  0.7 us (1%)
    all_to_all x2, blocking collectives, exchange(): return lax.all_to_all(blocks, axes, 0, 0, tiled=True)  19.9 us
    pallas_call x10, Pallas kernels, run(): pl.pallas_call(kernel, out_shape=outs, in_specs=specs, out_specs=[pl.Bloc...  17.9 us
    all_to_all x2, waiting for transfers between devices, exchange(): return lax.all_to_all(blocks, axes, 0, 0, tiled=True)  13.4 us
    all_to_all x2, starting transfers between devices, exchange(): return lax.all_to_all(blocks, axes, 0, 0, tiled=True)  9.43 us
  transfers between devices with their start and end apart: 3, of which 2 were waited for; matrix products, arithmetic and copies ran while one was open for 0% of the time, Pallas kernels for 11%

commit v1 on v0

--- a/solution.py
+++ b/solution.py
@@ -14,9 +14,10 @@
 RIM = 128
 BAND = 24
 MEL_ROWS = 16
-FIRST = 24
-SUMS, EDGES, COLUMNS = 16, 19, 23
-SIDE = 96
+FIRST = 16
+SUMS, EDGES, COLUMNS = 8, 11, 15
+SIDE, FAR = 96, 112
+FAR_HOLDERS = 32
 TAPS = 576
 SECOND = 8
 
@@ -135,10 +136,10 @@
     def put(n, value):
         rows_out[pl.ds(n, devices, stride=FIRST), :] = jnp.broadcast_to(value, (devices, 128))
 
-    near = jnp.concatenate([x[0:4], x[rows - 4 :]], axis=0)
+    near = jnp.concatenate([x[0:2], x[rows - 2 :]], axis=0)
     near = jnp.concatenate([near[:, :128], near[:, 128:]], axis=0)
     for d in range(devices):
-        rows_out[FIRST * d : FIRST * d + 16, :] = near
+        rows_out[FIRST * d : FIRST * d + 8, :] = near
     put(COLUMNS, strip)
     copies[2].wait()
     _, chan, many, half = own.shape
@@ -148,14 +149,14 @@
     edges[0:chan] = g[:, 0, :]
     edges[chan:] = g[:, many - 1, :]
 
-    def spread_out(v):
-        if holders < devices:
-            v = jnp.concatenate([v, jnp.zeros((devices - holders, 128), F32)], axis=0)
+    def spread_out(v, held):
+        if held < devices:
+            v = jnp.concatenate([v, jnp.zeros((devices - held, 128), F32)], axis=0)
         return v
 
     for n in range(share):
-        put(EDGES + n, spread_out(edges[n * holders : (n + 1) * holders, :]))
-        put(EDGES + share + n, spread_out(edges[chan + n * holders : chan + (n + 1) * holders, :]))
+        put(EDGES + n, spread_out(edges[n * holders : (n + 1) * holders, :], holders))
+        put(EDGES + share + n, spread_out(edges[chan + n * holders : chan + (n + 1) * holders, :], holders))
     for n in range(2 * share, COLUMNS - EDGES):
         put(EDGES + n, jnp.zeros((1, 128), F32))
     end = iota((8, half), 0)
@@ -166,6 +167,7 @@
     source = iota((128, 128), 0)
     lane = iota((group, 128), 1)
     mine = lane // many == iota((group, 128), 0)
+    lane8, own8 = iota((8, 128), 1), iota((8, 128), 0)
     parts = three_parts(features)
     for n in range(2):
         side = jnp.zeros((holders, 128), F32)
@@ -175,7 +177,11 @@
             block = [columns[n : n + 1, 128 * q : 128 * (q + 1)] for q in range(first, first + holders * many // 128)]
             block = jnp.concatenate([jnp.where(mine, v, 0.0) for v in block], axis=0)
             side = side + dot(block.astype(BF16), move)
-        put(SUMS + n, spread_out(side) + parts[n])
+        far = x[2:4] if n == 0 else x[rows - 4 : rows - 2]
+        pieces = [far[r : r + 1, 128 * h : 128 * (h + 1)] for r in range(2) for h in range(2)]
+        pieces = jnp.concatenate([jnp.where(lane8 // 16 == own8, v, 0.0) for v in pieces], axis=0)
+        far = dot(pieces.astype(BF16), (iota((128, 128), 1) == FAR + source % 16).astype(BF16))
+        put(SUMS + n, spread_out(side, holders) + spread_out(far, FAR_HOLDERS) + parts[n])
     put(SUMS + 2, parts[2])
     out[...] = rows_out[...].reshape(out.shape).astype(BF16)
 
@@ -318,7 +324,7 @@
 
 
 def forward_one(recv, spec, pairs, singles, twice, w1, wf, params, masks, all_masks, edge_masks,
-                pre_two, payload, act, x3, stats, features_out, pre_one, got, strips, halo, rows_out):
+                pre_two, payload, act, x3, far_rim, stats, features_out, pre_one, got, strips, halo, rows_out):
     devices = recv.shape[0]
     n_mel, count = lax.axis_size("mel"), lax.axis_size("tm")
     rows = MEL_ROWS
@@ -343,11 +349,11 @@
             column = column + (pltpu.roll(part, rows * (k - c) % 128, 1) if k != c else part)
         strips[pl.ds(c, count, stride=8), :] = column
     at = pl.multiple_of(FIRST * (jnp.maximum(me_m - 1, 0) * count + me_t), 8)
-    above = got[pl.ds(at, 16), :] * (me_m > 0).astype(F32)
+    above = got[pl.ds(at, 8), :] * (me_m > 0).astype(F32)
     at = pl.multiple_of(FIRST * (jnp.minimum(me_m + 1, n_mel - 1) * count + me_t), 8)
-    below = got[pl.ds(at, 16), :] * (me_m < n_mel - 1).astype(F32)
-    above = jnp.concatenate([above[4:8], above[12:16]], axis=1)
-    below = jnp.concatenate([below[0:4], below[8:12]], axis=1)
+    below = got[pl.ds(at, 8), :] * (me_m < n_mel - 1).astype(F32)
+    above = jnp.concatenate([above[2:4], above[6:8]], axis=1)
+    below = jnp.concatenate([below[0:2], below[4:6]], axis=1)
     own = spec[0].astype(F32) * usable[:, :frame_dev]
     at = pl.multiple_of(8 * jnp.minimum(me_t + 1, count - 1), 8)
     after = strips[pl.ds(at, 8), :][:, :mels] * (me_t + 1 < count).astype(F32)
@@ -360,7 +366,11 @@
     halo[mels : mels + 8] = jnp.zeros((8, RIM), F32)
     halo[4 : mels + 4] = dot(sides, place.astype(BF16), ((0,), (0,)))
     rim = halo[pl.ds(pl.multiple_of(me_m * rows, 8), BAND), :]
-    near = jnp.concatenate([jnp.concatenate([above, own, below], axis=0), rim], axis=1)
+    far_rim[...] = rim
+    row = iota((BAND, RIM), 0)
+    rim = jnp.where((row >= 2) & (row < BAND - 2), rim, 0.0)
+    blank = jnp.zeros((2, frame_dev), F32)
+    near = jnp.concatenate([jnp.concatenate([blank, above, own, below, blank], axis=0), rim], axis=1)
     x3[...] = jnp.concatenate(
         [
             pltpu.roll(near, 1, 1) * behind,
@@ -383,10 +393,10 @@
     def edge_row(k, n):
         first = FIRST * k * count + n
         return jnp.concatenate(
-            [got[pl.ds(first, count, stride=FIRST), :], got[pl.ds(first + 8, count, stride=FIRST), :]], axis=1
+            [got[pl.ds(first, count, stride=FIRST), :], got[pl.ds(first + 4, count, stride=FIRST), :]], axis=1
         )
 
-    edge_rows = [[edge_row(k, n) for n in (0, 1, 6, 7)] for k in range(n_mel)]
+    edge_rows = [[edge_row(k, n) for n in range(4)] for k in range(n_mel)]
     zero = jnp.zeros((count, frame_dev), F32)
     rows_of = [[], [], []]
     for k, (top, second, fore, bottom) in enumerate(edge_rows):
@@ -480,13 +490,17 @@
         put(n, jnp.zeros((1, 128), F32))
     lane = iota((devices, 128), 1)
     tm = iota((devices, 128), 0) % count
-    lefts = jnp.where(lane >= SIDE, every(SUMS), 0.0)
-    rights = jnp.where(lane >= SIDE, every(SUMS + 1), 0.0)
+    at_side = (lane >= SIDE) & (lane < FAR)
+    lefts = jnp.where(at_side, every(SUMS), 0.0)
+    rights = jnp.where(at_side, every(SUMS + 1), 0.0)
     beside = jnp.zeros((devices, 128), F32)
     for n, step in enumerate((0, count, -count)):
         one = jnp.where(tm > 0, moved_rows(rights, step + 1), 0.0)
         two = jnp.where(tm < count - 1, moved_rows(lefts, step - 1), 0.0)
         beside = beside + pltpu.roll(one, (32 * n - SIDE) % 128, 1) + pltpu.roll(two, (32 * n + 16 - SIDE) % 128, 1)
+    outer = jnp.where(lane >= FAR, moved_rows(every(SUMS + 1), count), 0.0)
+    beside = beside + pltpu.roll(outer, 128 - 16, 1)
+    beside = beside + jnp.where(lane >= FAR, moved_rows(every(SUMS), -count), 0.0)
     put(SECOND - 1, beside)
     first = jnp.sum(first, axis=1, keepdims=True)
     second = jnp.sum(second, axis=1, keepdims=True)
@@ -575,7 +589,7 @@
     sent_half[...] = halved[1 - core]
 
 
-def around(recv, pre_two, act, w1, wf, x3, stats_one, masks, stats, pre_ring, ring, rim, pairs,
+def around(recv, pre_two, act, w1, wf, x3, far_rim, stats_one, masks, stats, pre_ring, ring, rim, pairs,
            sides, up, got, beyond, more):
     devices = recv.shape[0]
     got[...] = recv[:, 0:SECOND, :].astype(F32).reshape(devices * SECOND, 128)
@@ -586,10 +600,34 @@
     chan = pre_two.shape[0] // rows
     usable = masks[0:1]
     low_masks = [masks[n : n + 1].astype(BF16) for n in range(3)]
+    pieces = got[pl.ds(SECOND - 1, devices, stride=SECOND), :][:FAR_HOLDERS].astype(BF16)
+    source = iota((128, 128), 0)
+    lane = iota((FAR_HOLDERS, 128), 1)
+    mine = lane // 16 == iota((FAR_HOLDERS, 128), 0) % 8
+    outer = []
+    for first in (SIDE, FAR):
+        place = (source - first == iota((128, 128), 1) % 16).astype(BF16)
+        v = jnp.where(mine, dot(pieces, place), 0.0)
+        v = [jnp.sum(v[8 * n : 8 * n + 8], axis=0, keepdims=True) for n in range(4)]
+        outer += [jnp.concatenate(v[2 * r : 2 * r + 2], axis=1) for r in range(2)]
+    blank = jnp.zeros((BAND - 4, frame_dev), F32)
+    far = jnp.concatenate(outer[:2] + [blank] + outer[2:], axis=0)
+    row = iota((BAND, RIM), 0)
+    far = jnp.concatenate([far, jnp.where((row < 2) | (row >= BAND - 2), far_rim[...], 0.0)], axis=1)
+    far = jnp.concatenate(
+        [
+            pltpu.roll(far, 1, 1) * masks[1:2],
+            far,
+            pltpu.roll(far, wide - 1, 1) * masks[2:3],
+            jnp.zeros((128 - 3 * BAND, wide), F32),
+        ],
+        axis=0,
+    )
+    x_all = (x3[...].astype(F32) + far).astype(BF16)
     scale = jnp.broadcast_to(stats_one[chan + 16 :, 0:1], (chan, wide))
     shift = jnp.broadcast_to(stats_one[chan + 16 :, 1:2], (chan, wide))
     for h, start in enumerate((0, rows + 4)):
-        pre_one = dot(w1[start * chan : (start + 2) * chan, :], x3[...])
+        pre_one = dot(w1[start * chan : (start + 2) * chan, :], x_all)
         for n in range(2):
             value, _ = silu_halves(pre_one[n * chan : (n + 1) * chan] * scale + shift)
             value = value * row_valid(start + n - 3, rows)
@@ -990,13 +1028,14 @@
         hbm=7,
         apart=(3,),
     )
-    pre_two, payload, act, x3, stats_one, features = run(
+    pre_two, payload, act, x3, far_rim, stats_one, features = run(
         forward_one,
         [
             kept((rows * chan, wide)),
             kept((devices, SECOND, 128), BF16),
             kept((ext * 3 * chan, wide), BF16),
             kept((128, wide), BF16),
+            kept((BAND, RIM)),
             kept((2 * chan + 16, 128)),
             kept((8, 128)),
         ],
@@ -1059,6 +1098,7 @@
         w1,
         wf,
         x3,
+        far_rim,
         stats_one,
         masks,
         stats_two,

time: 62.2 us -> 61 us (0.981)
  waiting for transfers between devices: 13.4 us -> 12.4 us
    all_to_all x2, waiting for transfers between devices: 13.4 us -> 12.4 us  [exchange(): return lax.all_to_all(blocks, axes, 0, 0, tiled=True)]
where the time goes in v1:
time: 61 us; the launch traced here: 60.7 us
  blocking collectives  19.5 us (32%)
  Pallas kernels  18.3 us (30%)
  waiting for transfers between devices  12.4 us (20%)
  starting transfers between devices  9.88 us (16%)
  between operations  0.7 us (1%)
    all_to_all x2, blocking collectives, exchange(): return lax.all_to_all(blocks, axes, 0, 0, tiled=True)  19.5 us
    pallas_call x10, Pallas kernels, run(): pl.pallas_call(kernel, out_shape=outs, in_specs=specs, out_specs=[pl.Bloc...  18.3 us
    all_to_all x2, waiting for transfers between devices, exchange(): return lax.all_to_all(blocks, axes, 0, 0, tiled=True)  12.4 us
    all_to_all x2, starting transfers between devices, exchange(): return lax.all_to_all(blocks, axes, 0, 0, tiled=True)  9.43 us
  transfers between devices with their start and end apart: 3, of which 2 were waited for; matrix products, arithmetic and copies ran while one was open for 0% of the time, Pallas kernels for 11%

profile of v1, /device:TPU:1, one launch (start us, length us, event | category | flops | bytes accessed | tf_op | source)
XLA Modules:
  0.0 60.7 jit_solution(4933902544043672233)
XLA Ops:
  0.6 2.0 %shard_map.152 = (bf16[32,16,128]{2,1,0:T(8,128)(2,1)}, bf16[1,64,8,128]{3,2,1,0:T(8,128)(2,1)S(1)}, bf16[1,16,256]{2,1,0:T(8,128)(2,1)S(1)}, f32[8,384]{1,0:T(8,128)S(1)}) custom-call(bf16[1,16,256]{2,1,0:T(8,128)(2,1)} %spec_hbm.1, bf16[1,64,8,128]{3,2,1,0:T(8,128)(2,1)} %grad_hbm.1, s32[1,4]{1,0:T(1,128)} %bounds_hbm.3), custom_call_target="tpu_custom_call" | custom-call | flops 100000000 | bytes 4000000 | tf_op jit(solution)/shard_map/pallas_call | solution.py:933
  2.7 7.1 %all-to-all-start = ((bf16[32,16,128]{2,1,0:T(8,128)(2,1)}), bf16[32,16,128]{2,1,0:T(8,128)(2,1)S(1)}, u32[]{:S(2)}, u32[]{:S(2)}) async-start(bf16[32,16,128]{2,1,0:T(8,128)(2,1)} %get-tuple-element.55), calls=%async_computation | async-start | bytes 262144 | tf_op jit(solution)/shard_map/all_to_all | solution.py:957
  9.8 2.1 %shard_map.153 = (bf16[128,768]{1,0:T(8,128)(2,1)S(1)}, bf16[128,768]{1,0:T(8,128)(2,1)S(1)}, bf16[1408,128]{1,0:T(8,128)(2,1)S(1)}, bf16[48,1152]{1,0:T(8,128)(...) custom-call(bf16[1,64,8,128]{3,2,1,0:T(8,128)(2,1)S(1)} %get-tuple-e, ...), custom_call_target="tpu_custom_call" | custom-call | flops 100000000 | bytes 4000000 | tf_op jit(solution)/shard_map/pallas_call | solution.py:933
  11.9 6.1 %all-to-all-done.recv = bf16[32,16,128]{2,1,0:T(8,128)(2,1)S(1)} async-done(((bf16[32,16,128]{2,1,0:T(8,128)(2,1)}), bf16[32,16,128]{2,1,0:T(8,128)(2,1)S(1)}, u32[]{:S(2)}, u32[]{:S(2)}) %all-to-all-start) | async-done | bytes 131104 | tf_op jit(solution)/shard_map/all_to_all | solution.py:957
  18.0 2.5 %shard_map.154 = (f32[1024,384]{1,0:T(8,128)S(1)}, bf16[32,8,128]{2,1,0:T(8,128)(2,1)S(1)}, bf16[4224,384]{1,0:T(8,128)(2,1)S(1)}, bf16[128,384]{1,0:T(8,128)(2,...) custom-call(bf16[32,16,128]{2,1,0:T(8,128)(2,1)S(1)} %all-to-all-done.recv, ...), custom_call_target="tpu_custom_call" | custom-call | flops 100000000 | bytes 4000000 | tf_op jit(solution)/shard_map/pallas_call | solution.py:933
  20.5 8.9 %all_to_all.20.recv = bf16[32,8,128]{2,1,0:T(8,128)(2,1)S(1)} all-to-all(bf16[32,8,128]{2,1,0:T(8,128)(2,1)S(1)} %get-tuple-element.67), channel_id=1, replica_groups=mesh['mel'=4,'tm'=8] {'mel','tm'}, dimensions={0} | all-to-all | bytes 131072 | tf_op jit(solution)/shard_map/all_to_all | solution.py:957
  29.4 2.2 %shard_map.155 = (f32[1024,256]{1,0:T(8,128)S(1)}, f32[320,128]{1,0:T(8,128)S(1)}, f32[320,128]{1,0:T(8,128)S(1)}, f32[8,128]{1,0:T(8,128)S(1)}, f32[72,128]{1,0:T(8,128)S(1)}) custom-call(bf16[32,8,128]{2,1,0:T(8,128)(2,1)S(1)} %all_to_all.20.recv, f32[1024,384]{1,0:T(8,128)S(1)} %get-tuple-element.68.pre_two, bf16[4224,384]{1,0:T(8,128)(2,1)S(1)} %get-tuple-element.69.act, ...), custom_call_target="tpu_custom_call" | custom-call | flops 100000000 | bytes 4000000 | tf_op jit(solution)/shard_map/pallas_call | solution.py:933
  31.7 0.5 collective-permute-start
  32.1 1.4 %shard_map.156 = (f32[256,384]{1,0:T(8,128)S(1)}, f32[256,384]{1,0:T(8,128)S(1)}, f32[1024,128]{1,0:T(8,128)S(1)}, f32[512,256]{1,0:T(8,128)S(1)}) custom-call(bf16[32,8,128]{2,1,0:T(8,128)(2,1)S(1)} %all_to_all.20.recv, f32[1024,384]{1,0:T(8,128)S(1)} %get-tuple-element.68.pre_two, bf16[4224,384]{1,0:T(8,128)(2,1)S(1)} %get-tuple-element.69.act, ...), custom_call_target="tpu_custom_call" | custom-call | flops 100000000 | bytes 4000000 | tf_op jit(solution)/shard_map/pallas_call | solution.py:933
  33.6 0.0 collective-permute-done.received
  33.6 10.6 %all_to_all.21 = f32[352,1,128]{2,1,0:T(1,128)S(1)} all-to-all(f32[352,1,128]{2,1,0:T(1,128)S(1)} %bitcast.26), channel_id=1, replica_groups=mesh['mel'=4,'tm'=8] {'mel','tm'}, dimensions={0} | all-to-all | bytes 360448 | tf_op jit(solution)/shard_map/all_to_all | solution.py:957
  44.2 3.1 %shard_map.158 = (bf16[1280,384]{1,0:T(8,128)(2,1)S(1)}, bf16[1024,256]{1,0:T(8,128)(2,1)S(1)}, f32[448,128]{1,0:T(8,128)}, f32[8,128]{1,0:T(8,128)S(1)}) custom-call(f32[352,128]{1,0:T(8,128)S(1)} %bitcast.25, f32[1024,384]{1,0:T(8,128)S(1)} %get-tuple-element.68.pre_two, f32[256,384]{1,0:T(8,128)S(1)} %get-tuple-element.79.pre_ring, ...), custom_call_target="tpu_custom_call" | custom-call | flops 100000000 | bytes 4000000 | tf_op jit(solution)/shard_map/pallas_call | solution.py:933
  47.2 2.3 %all-to-all-start.3 = ((f32[448,1,128]{2,1,0:T(1,128)}), f32[448,1,128]{2,1,0:T(1,128)S(1)}, u32[]{:S(2)}, u32[]{:S(2)}) async-start(f32[448,1,128]{2,1,0:T(1,128)} %bitcast.11), calls=%async_computation.3 | async-start | bytes 458752 | tf_op jit(solution)/shard_map/all_to_all | solution.py:957
  49.6 1.3 %shard_map.159 = (bf16[1,64,8,128]{3,2,1,0:T(8,128)(2,1)}, f32[1,64]{1,0:T(1,128)}, f32[1,64]{1,0:T(1,128)}) custom-call(f32[8,128]{1,0:T(8,128)S(1)} %get-tuple-element.83.totals, f32[512,256]{1,0:T(8,128)S(1)} %get-tuple-element.84.pairs), custom_call_target="tpu_custom_call" | custom-call | flops 100000000 | bytes 4000000 | tf_op jit(solution)/shard_map/pallas_call | solution.py:933
  50.8 2.2 %shard_map.160 = (f32[48,384]{1,0:T(8,128)S(1)}, bf16[48,1152]{1,0:T(8,128)(2,1)S(1)}, f32[32,64]{1,0:T(8,128)S(1)}) custom-call(bf16[1280,384]{1,0:T(8,128)(2,1)S(1)} %get-tuple-element.89.grad, bf16[1024,256]{1,0:T(8,128)(2,1)S(1)} %get-tuple-element.90.own_low, bf16[1408,128]{1,0:T(8,128)(2,1)S(1)} %get-tuple-element.61.w1, ...), custom_call_target="tpu_custom_call" | custom-call | flops 100000000 | bytes 4000000 | tf_op jit(solution)/shard_map/pallas_call | solution.py:933
  53.0 6.2 %all-to-all-done.3 = f32[448,1,128]{2,1,0:T(1,128)S(1)} async-done(((f32[448,1,128]{2,1,0:T(1,128)}), f32[448,1,128]{2,1,0:T(1,128)S(1)}, u32[]{:S(2)}, u32[]{:S(2)}) %all-to-all-start.3) | async-done | bytes 229408 | tf_op jit(solution)/shard_map/all_to_all | solution.py:957
  59.3 1.4 %shard_map.161 = (f32[1,16,256]{2,1,0:T(8,128)}, f32[3,3,64]{2,1,0:T(4,128)}, f32[9,64,64]{2,1,0:T(8,128)}, f32[1,64]{1,0:T(1,128)}, f32[1,64]{1,0:T(1,128)}) custom-call(f32[448,128]{1,0:T(8,128)S(1)} %bitcast.24, f32[8,128]{1,0:T(8,128)S(1)} %get-tuple-element.87.features, f32[144,128]{1,0:T(8,128)S(1)} %get-tuple-element.76.stats_one.stats, ...), custom_call_target="tpu_custom_call" | custom-call | flops 100000000 | bytes 4000000 | tf_op jit(solution)/shard_map/pallas_call | solution.py:933
  (1 shorter events, 0.0 us)
Async XLA Ops:
  2.7 15.3 %all-to-all-start = ((bf16[32,16,128]{2,1,0:T(8,128)(2,1)}), bf16[32,16,128]{2,1,0:T(8,128)(2,1)S(1)}, u32[]{:S(2)}, u32[]{:S(2)}) async-start(bf16[32,16,128]{2,1,0:T(8,128)(2,1)} %get-tuple-element.55), calls=%async_computation | async-start | bytes 262144 | tf_op jit(solution)/shard_map/all_to_all | solution.py:957
  31.7 1.9 %collective-permute-start = (f32[320,128]{1,0:T(8,128)S(1)}, f32[320,128]{1,0:T(8,128)S(1)}, u32[]{:S(2)}, u32[]{:S(2)}) collective-permute-start(f32[320,128]{1,0:T(8,128)S(1)} %get-tuple-element.72), channel_id=1, source_target_pairs={{0,1},{1,0},{2,3},{3,2},{4,5},{5,4},{6,7},{7,6},{8,9},{9,8},{10,11... | collective-permute-start | bytes 491528 | tf_op jit(solution)/shard_map/ppermute | solution.py:1084
  47.2 12.0 %all-to-all-start.3 = ((f32[448,1,128]{2,1,0:T(1,128)}), f32[448,1,128]{2,1,0:T(1,128)S(1)}, u32[]{:S(2)}, u32[]{:S(2)}) async-start(f32[448,1,128]{2,1,0:T(1,128)} %bitcast.11), calls=%async_computation.3 | async-start | bytes 458752 | tf_op jit(solution)/shard_map/all_to_all | solution.py:957

commit v2 on v1

--- a/solution.py
+++ b/solution.py
@@ -95,8 +95,8 @@
 
 
 def pack(spec_hbm, grad_hbm, bounds_hbm, out, own, spec, masks, bounds, edges, rows_out, sems):
-    copies = start_all((bounds_hbm, bounds), (spec_hbm, spec), (grad_hbm, own), sems=sems)
-    copies[0].wait()
+    copies = start_all((spec_hbm, spec), (bounds_hbm, bounds), (grad_hbm, own), sems=sems)
+    copies[1].wait()
     wide = masks.shape[1]
     frame_dev = wide - RIM
     devices = out.shape[0]
@@ -110,7 +110,7 @@
         list(found) + [jnp.full((1, wide), 1.0) * pixels, jnp.zeros((4, wide), F32)], axis=0
     )
     usable, behind, ahead = (m[:, :frame_dev] for m in found)
-    copies[1].wait()
+    copies[0].wait()
     x = spec[0].astype(F32) * usable
     lane = iota((1, frame_dev), 1)
     row = iota((rows, 1), 0)
@@ -520,9 +520,8 @@
 
 
 def backward_scaled(recv, pre_two, act, own_rows, params, masks,
-                    grad, kept_half, sent_half, totals, stats, up, right, got, halved):
+                    grad, kept_half, sent_half, totals, stats, up, right, halved):
     devices = recv.shape[0]
-    got[...] = recv[:, 0:SECOND, :].astype(F32).reshape(devices * SECOND, 128)
     chan = params.shape[1]
     half = own_rows.shape[1]
     frame_dev = 2 * half
@@ -530,8 +529,10 @@
     up[...] = dot(own_rows[...], spreading(half))
     usable = masks[0:1, :frame_dev]
     total = masks[3:4, 0:1]
-    sums = [got[pl.ds(n, devices, stride=SECOND), :] for n in range(3)]
-    sums = jnp.sum(sums[0] + sums[1] + sums[2], axis=0, keepdims=True)
+    sums = [recv[d].astype(F32) for d in range(devices)]
+    while len(sums) > 1:
+        sums = [a + b for a, b in zip(sums[0::2], sums[1::2])]
+    sums = jnp.sum(sums[0][0:3], axis=0, keepdims=True)
     mean = to_column(sums, chan) / total
     inv = lax.rsqrt(to_column(sums, chan, chan) / total - mean * mean + 1e-05)
     scale = 0.5 * to_column(params[2:3], chan) * inv
@@ -643,7 +644,7 @@
     def every(n):
         return got[pl.ds(n, devices, stride=SECOND), :]
 
-    beside = every(SECOND - 1)[:holders]
+    beside = 0.25 * every(SECOND - 1)[:holders]
     lane = iota((holders, RIM), 1)
     for n in range(share):
         first = n * holders
@@ -652,7 +653,7 @@
         for r in range(many + 2):
             at = many * n + (r if r < many else 32 + many - 1 if r == many else 64)
             left, right_of = beside[:, at : at + 1], beside[:, at + 16 : at + 17]
-            side = jnp.where(lane >= RIM - 2, 0.25 * left, jnp.where(lane < 2, 0.25 * right_of, 0.0))
+            side = jnp.where(lane >= RIM - 2, left, jnp.where(lane < 2, right_of, 0.0))
             sides[r * chan + first : r * chan + first + holders, :] = side
     up[...] = dot(beyond[...].astype(BF16), spreading(frame_dev // 2))
     scale = jnp.broadcast_to(stats[0:chan, 2:3], (chan, wide))
@@ -1071,7 +1072,6 @@
         [
             pltpu.VMEM((rows // 2 * chan, frame_dev), F32),
             pltpu.VMEM((3 * chan + 16, rows * frame_dev), BF16),
-            pltpu.VMEM((devices * SECOND, 128), F32),
             pltpu.VMEM((2, TAPS // 2 + devices, 128), F32),
         ],
         recv,

time: 61 us -> 61.1 us (level)
  no operation moved by 1% of the time
where the time goes in v2:
time: 61.1 us; the launch traced here: 60.8 us
  blocking collectives  19.5 us (32%)
  Pallas kernels  18.4 us (30%)
  waiting for transfers between devices  12.4 us (20%)
  starting transfers between devices  9.87 us (16%)
  between operations  0.7 us (1%)
    all_to_all x2, blocking collectives, exchange(): return lax.all_to_all(blocks, axes, 0, 0, tiled=True)  19.5 us
    pallas_call x10, Pallas kernels, run(): pl.pallas_call(kernel, out_shape=outs, in_specs=specs, out_specs=[pl.Bloc...  18.4 us
    all_to_all x2, waiting for transfers between devices, exchange(): return lax.all_to_all(blocks, axes, 0, 0, tiled=True)  12.4 us
    all_to_all x2, starting transfers between devices, exchange(): return lax.all_to_all(blocks, axes, 0, 0, tiled=True)  9.43 us
  transfers between devices with their start and end apart: 3, of which 2 were waited for; matrix products, arithmetic and copies ran while one was open for 0% of the time, Pallas kernels for 11%

profile of v2, /device:TPU:1, one launch (start us, length us, event | category | flops | bytes accessed | tf_op | source)
XLA Modules:
  0.0 60.8 jit_solution(5328552116796798235)
XLA Ops:
  0.6 2.2 %shard_map.152 = (bf16[32,16,128]{2,1,0:T(8,128)(2,1)}, bf16[1,64,8,128]{3,2,1,0:T(8,128)(2,1)S(1)}, bf16[1,16,256]{2,1,0:T(8,128)(2,1)S(1)}, f32[8,384]{1,0:T(8,128)S(1)}) custom-call(bf16[1,16,256]{2,1,0:T(8,128)(2,1)} %spec_hbm.1, bf16[1,64,8,128]{3,2,1,0:T(8,128)(2,1)} %grad_hbm.1, s32[1,4]{1,0:T(1,128)} %bounds_hbm.3), custom_call_target="tpu_custom_call" | custom-call | flops 100000000 | bytes 4000000 | tf_op jit(solution)/shard_map/pallas_call | solution.py:934
  2.8 7.1 %all-to-all-start = ((bf16[32,16,128]{2,1,0:T(8,128)(2,1)}), bf16[32,16,128]{2,1,0:T(8,128)(2,1)S(1)}, u32[]{:S(2)}, u32[]{:S(2)}) async-start(bf16[32,16,128]{2,1,0:T(8,128)(2,1)} %get-tuple-element.55), calls=%async_computation | async-start | bytes 262144 | tf_op jit(solution)/shard_map/all_to_all | solution.py:958
  9.9 2.1 %shard_map.153 = (bf16[128,768]{1,0:T(8,128)(2,1)S(1)}, bf16[128,768]{1,0:T(8,128)(2,1)S(1)}, bf16[1408,128]{1,0:T(8,128)(2,1)S(1)}, bf16[48,1152]{1,0:T(8,128)(...) custom-call(bf16[1,64,8,128]{3,2,1,0:T(8,128)(2,1)S(1)} %get-tuple-e, ...), custom_call_target="tpu_custom_call" | custom-call | flops 100000000 | bytes 4000000 | tf_op jit(solution)/shard_map/pallas_call | solution.py:934
  12.0 6.1 %all-to-all-done.recv = bf16[32,16,128]{2,1,0:T(8,128)(2,1)S(1)} async-done(((bf16[32,16,128]{2,1,0:T(8,128)(2,1)}), bf16[32,16,128]{2,1,0:T(8,128)(2,1)S(1)}, u32[]{:S(2)}, u32[]{:S(2)}) %all-to-all-start) | async-done | bytes 131104 | tf_op jit(solution)/shard_map/all_to_all | solution.py:958
  18.1 2.5 %shard_map.154 = (f32[1024,384]{1,0:T(8,128)S(1)}, bf16[32,8,128]{2,1,0:T(8,128)(2,1)S(1)}, bf16[4224,384]{1,0:T(8,128)(2,1)S(1)}, bf16[128,384]{1,0:T(8,128)(2,...) custom-call(bf16[32,16,128]{2,1,0:T(8,128)(2,1)S(1)} %all-to-all-done.recv, ...), custom_call_target="tpu_custom_call" | custom-call | flops 100000000 | bytes 4000000 | tf_op jit(solution)/shard_map/pallas_call | solution.py:934
  20.6 8.9 %all_to_all.20.recv = bf16[32,8,128]{2,1,0:T(8,128)(2,1)S(1)} all-to-all(bf16[32,8,128]{2,1,0:T(8,128)(2,1)S(1)} %get-tuple-element.67), channel_id=1, replica_groups=mesh['mel'=4,'tm'=8] {'mel','tm'}, dimensions={0} | all-to-all | bytes 131072 | tf_op jit(solution)/shard_map/all_to_all | solution.py:958
  29.5 2.2 %shard_map.155 = (f32[1024,256]{1,0:T(8,128)S(1)}, f32[320,128]{1,0:T(8,128)S(1)}, f32[320,128]{1,0:T(8,128)S(1)}, f32[8,128]{1,0:T(8,128)S(1)}, f32[72,128]{1,0:T(8,128)S(1)}) custom-call(bf16[32,8,128]{2,1,0:T(8,128)(2,1)S(1)} %all_to_all.20.recv, f32[1024,384]{1,0:T(8,128)S(1)} %get-tuple-element.68.pre_two, bf16[4224,384]{1,0:T(8,128)(2,1)S(1)} %get-tuple-element.69.act, ...), custom_call_target="tpu_custom_call" | custom-call | flops 100000000 | bytes 4000000 | tf_op jit(solution)/shard_map/pallas_call | solution.py:934
  31.8 0.4 collective-permute-start
  32.2 1.4 %shard_map.156 = (f32[256,384]{1,0:T(8,128)S(1)}, f32[256,384]{1,0:T(8,128)S(1)}, f32[1024,128]{1,0:T(8,128)S(1)}, f32[512,256]{1,0:T(8,128)S(1)}) custom-call(bf16[32,8,128]{2,1,0:T(8,128)(2,1)S(1)} %all_to_all.20.recv, f32[1024,384]{1,0:T(8,128)S(1)} %get-tuple-element.68.pre_two, bf16[4224,384]{1,0:T(8,128)(2,1)S(1)} %get-tuple-element.69.act, ...), custom_call_target="tpu_custom_call" | custom-call | flops 100000000 | bytes 4000000 | tf_op jit(solution)/shard_map/pallas_call | solution.py:934
  33.7 0.0 collective-permute-done.received
  33.7 10.6 %all_to_all.21 = f32[352,1,128]{2,1,0:T(1,128)S(1)} all-to-all(f32[352,1,128]{2,1,0:T(1,128)S(1)} %bitcast.26), channel_id=1, replica_groups=mesh['mel'=4,'tm'=8] {'mel','tm'}, dimensions={0} | all-to-all | bytes 360448 | tf_op jit(solution)/shard_map/all_to_all | solution.py:958
  44.3 3.1 %shard_map.158 = (bf16[1280,384]{1,0:T(8,128)(2,1)S(1)}, bf16[1024,256]{1,0:T(8,128)(2,1)S(1)}, f32[448,128]{1,0:T(8,128)}, f32[8,128]{1,0:T(8,128)S(1)}) custom-call(f32[352,128]{1,0:T(8,128)S(1)} %bitcast.25, f32[1024,384]{1,0:T(8,128)S(1)} %get-tuple-element.68.pre_two, f32[256,384]{1,0:T(8,128)S(1)} %get-tuple-element.79.pre_ring, ...), custom_call_target="tpu_custom_call" | custom-call | flops 100000000 | bytes 4000000 | tf_op jit(solution)/shard_map/pallas_call | solution.py:934
  47.4 2.3 %all-to-all-start.3 = ((f32[448,1,128]{2,1,0:T(1,128)}), f32[448,1,128]{2,1,0:T(1,128)S(1)}, u32[]{:S(2)}, u32[]{:S(2)}) async-start(f32[448,1,128]{2,1,0:T(1,128)} %bitcast.11), calls=%async_computation.3 | async-start | bytes 458752 | tf_op jit(solution)/shard_map/all_to_all | solution.py:958
  49.7 1.3 %shard_map.159 = (bf16[1,64,8,128]{3,2,1,0:T(8,128)(2,1)}, f32[1,64]{1,0:T(1,128)}, f32[1,64]{1,0:T(1,128)}) custom-call(f32[8,128]{1,0:T(8,128)S(1)} %get-tuple-element.83.totals, f32[512,256]{1,0:T(8,128)S(1)} %get-tuple-element.84.pairs), custom_call_target="tpu_custom_call" | custom-call | flops 100000000 | bytes 4000000 | tf_op jit(solution)/shard_map/pallas_call | solution.py:934
  51.0 2.2 %shard_map.160 = (f32[48,384]{1,0:T(8,128)S(1)}, bf16[48,1152]{1,0:T(8,128)(2,1)S(1)}, f32[32,64]{1,0:T(8,128)S(1)}) custom-call(bf16[1280,384]{1,0:T(8,128)(2,1)S(1)} %get-tuple-element.89.grad, bf16[1024,256]{1,0:T(8,128)(2,1)S(1)} %get-tuple-element.90.own_low, bf16[1408,128]{1,0:T(8,128)(2,1)S(1)} %get-tuple-element.61.w1, ...), custom_call_target="tpu_custom_call" | custom-call | flops 100000000 | bytes 4000000 | tf_op jit(solution)/shard_map/pallas_call | solution.py:934
  53.1 6.2 %all-to-all-done.3 = f32[448,1,128]{2,1,0:T(1,128)S(1)} async-done(((f32[448,1,128]{2,1,0:T(1,128)}), f32[448,1,128]{2,1,0:T(1,128)S(1)}, u32[]{:S(2)}, u32[]{:S(2)}) %all-to-all-start.3) | async-done | bytes 229408 | tf_op jit(solution)/shard_map/all_to_all | solution.py:958
  59.4 1.4 %shard_map.161 = (f32[1,16,256]{2,1,0:T(8,128)}, f32[3,3,64]{2,1,0:T(4,128)}, f32[9,64,64]{2,1,0:T(8,128)}, f32[1,64]{1,0:T(1,128)}, f32[1,64]{1,0:T(1,128)}) custom-call(f32[448,128]{1,0:T(8,128)S(1)} %bitcast.24, f32[8,128]{1,0:T(8,128)S(1)} %get-tuple-element.87.features, f32[144,128]{1,0:T(8,128)S(1)} %get-tuple-element.76.stats_one.stats, ...), custom_call_target="tpu_custom_call" | custom-call | flops 100000000 | bytes 4000000 | tf_op jit(solution)/shard_map/pallas_call | solution.py:934
  (1 shorter events, 0.0 us)
Async XLA Ops:
  2.8 15.3 %all-to-all-start = ((bf16[32,16,128]{2,1,0:T(8,128)(2,1)}), bf16[32,16,128]{2,1,0:T(8,128)(2,1)S(1)}, u32[]{:S(2)}, u32[]{:S(2)}) async-start(bf16[32,16,128]{2,1,0:T(8,128)(2,1)} %get-tuple-element.55), calls=%async_computation | async-start | bytes 262144 | tf_op jit(solution)/shard_map/all_to_all | solution.py:958
  31.8 1.9 %collective-permute-start = (f32[320,128]{1,0:T(8,128)S(1)}, f32[320,128]{1,0:T(8,128)S(1)}, u32[]{:S(2)}, u32[]{:S(2)}) collective-permute-start(f32[320,128]{1,0:T(8,128)S(1)} %get-tuple-element.72), channel_id=1, source_target_pairs={{0,1},{1,0},{2,3},{3,2},{4,5},{5,4},{6,7},{7,6},{8,9},{9,8},{10,11... | collective-permute-start | bytes 491528 | tf_op jit(solution)/shard_map/ppermute | solution.py:1084
  47.4 12.0 %all-to-all-start.3 = ((f32[448,1,128]{2,1,0:T(1,128)}), f32[448,1,128]{2,1,0:T(1,128)S(1)}, u32[]{:S(2)}, u32[]{:S(2)}) async-start(f32[448,1,128]{2,1,0:T(1,128)} %bitcast.11), calls=%async_computation.3 | async-start | bytes 458752 | tf_op jit(solution)/shard_map/all_to_all | solution.py:958

commit v3 on v2

--- a/solution.py
+++ b/solution.py
@@ -18,6 +18,7 @@
 SUMS, EDGES, COLUMNS = 8, 11, 15
 SIDE, FAR = 96, 112
 FAR_HOLDERS = 32
+LAST = 24
 TAPS = 576
 SECOND = 8
 
@@ -95,8 +96,8 @@
 
 
 def pack(spec_hbm, grad_hbm, bounds_hbm, out, own, spec, masks, bounds, edges, rows_out, sems):
-    copies = start_all((spec_hbm, spec), (bounds_hbm, bounds), (grad_hbm, own), sems=sems)
-    copies[1].wait()
+    copies = start_all((bounds_hbm, bounds), (spec_hbm, spec), (grad_hbm, own), sems=sems)
+    copies[0].wait()
     wide = masks.shape[1]
     frame_dev = wide - RIM
     devices = out.shape[0]
@@ -110,7 +111,7 @@
         list(found) + [jnp.full((1, wide), 1.0) * pixels, jnp.zeros((4, wide), F32)], axis=0
     )
     usable, behind, ahead = (m[:, :frame_dev] for m in found)
-    copies[0].wait()
+    copies[1].wait()
     x = spec[0].astype(F32) * usable
     lane = iota((1, frame_dev), 1)
     row = iota((rows, 1), 0)
@@ -520,7 +521,7 @@
 
 
 def backward_scaled(recv, pre_two, act, own_rows, params, masks,
-                    grad, kept_half, sent_half, totals, stats, up, right, halved):
+                    grad, kept_half, sent_half, totals, stats, pairs, up, right, halved):
     devices = recv.shape[0]
     chan = params.shape[1]
     half = own_rows.shape[1]
@@ -552,7 +553,11 @@
     for m in range(rows):
         at = slice(m * chan, (m + 1) * chan)
         pre = pre_two[at, :frame_dev]
-        _, slope = silu_halves(pre * scale + shift)
+        value, slope = silu_halves(pre * scale + shift)
+        value = value * usable
+        both = value if m % 2 == 0 else both + value
+        if m % 2:
+            pairs[m // 2 * chan : (m // 2 + 1) * chan, :] = both
         g = up[m // 2 * chan : (m // 2 + 1) * chan, :] * slope * mask
         grad[at, :] = g
         normed = (pre - mean) * inv
@@ -590,7 +595,7 @@
     sent_half[...] = halved[1 - core]
 
 
-def around(recv, pre_two, act, w1, wf, x3, far_rim, stats_one, masks, stats, pre_ring, ring, rim, pairs,
+def around(recv, pre_two, act, w1, wf, x3, far_rim, stats_one, masks, stats, pre_ring, ring, rim,
            sides, up, got, beyond, more):
     devices = recv.shape[0]
     got[...] = recv[:, 0:SECOND, :].astype(F32).reshape(devices * SECOND, 128)
@@ -669,17 +674,11 @@
         )
         _, slope = silu_halves(pre_ring[n * chan : (n + 1) * chan, :] * scale + shift)
         ring[n * chan : (n + 1) * chan, :] = upstream * slope * (usable * (0.5 * row_valid(m, rows)))
-    both = None
     for m in range(rows):
         at = slice(m * chan, (m + 1) * chan)
         _, slope = silu_halves(pre_two[at, frame_dev:] * scale[:, frame_dev:] + shift[:, frame_dev:])
         upstream = sides[m // 2 * chan : (m // 2 + 1) * chan, :]
         rim[m * chan : (m + 1) * chan, :] = upstream * slope * (0.5 * usable[:, frame_dev:])
-        value, _ = silu_halves(pre_two[at, :frame_dev] * scale[:, :frame_dev] + shift[:, :frame_dev])
-        value = value * usable[:, :frame_dev]
-        both = value if m % 2 == 0 else both + value
-        if m % 2:
-            pairs[m // 2 * chan : (m // 2 + 1) * chan, :] = both
 
 
 def pack_sums(kept_half, received, totals, after, payload):
@@ -717,7 +716,7 @@
     usable = masks[0:1]
     behind, ahead = (masks[n : n + 1].astype(BF16) for n in (1, 2))
     total = masks[3:4, 0:1]
-    devices = payload.shape[0] // 14
+    devices = payload.shape[0]
     pre_one[...] = dot(w1[3 * chan : (rows + 3) * chan], x3[:, :frame_dev])
 
     even, odd = summed_blocks(recv, devices, 2)
@@ -791,10 +790,9 @@
     places = [BAND * j + i for i in range(3) for j in range(3)] + [3 * BAND]
     rows10 = jnp.concatenate([table[n : n + 1] for n in places], axis=0)
     sums = jnp.concatenate([rows10[0:5], rows10[5:10]], axis=1)
-    block = jnp.concatenate([sums, mine], axis=0)
-    block = jnp.concatenate([block] * 4, axis=0)
-    for d in range(0, devices, 4):
-        payload[14 * d : 14 * (d + 4), :] = block
+    block = jnp.concatenate(list(three_parts(sums)) + [mine], axis=0).astype(BF16)
+    for d in range(devices):
+        payload[d] = block
 
 
 def transposed(grad, own_low, w1, wb, x3, stats, features, k1t, params, masks, ws_hbm,
@@ -859,7 +857,7 @@
 
 def finish(recv, features, stats, k1t, first, ws, w1, x3, normed_taps, params, masks,
            spec_hbm, kernel_one_hbm, kernel_two_hbm, gain_hbm, bias_hbm,
-           spec_grad, kernel_one, kernel_two, gain_out, bias_out, sems):
+           spec_grad, kernel_one, kernel_two, gain_out, bias_out, got, sems):
     chan = params.shape[1]
     rows = MEL_ROWS
     wide = x3.shape[1]
@@ -867,9 +865,11 @@
     usable, behind, ahead = (masks[n : n + 1] for n in range(3))
     total = masks[3:4, 0:1]
     gain = params[0:1]
-    count = recv.shape[0] // 14
+    count = recv.shape[0]
     share = half_share(count, 9 * chan)
-    sums = summed_blocks(recv, count)[0:5]
+    got[...] = recv[...].astype(F32).reshape(count * LAST, 128)
+    sums = summed_blocks(got, count)
+    sums = sums[0:5] + sums[5:10] + sums[10:15]
     ten = jnp.concatenate([sums[:, :chan], sums[:, chan:]], axis=0)
     bias_sum = ten[9:10]
     mean_l, inv_l = stats[chan : chan + 1, :chan], stats[chan + 8 : chan + 9, :chan]
@@ -891,7 +891,7 @@
         return v[:many] + v[many:]
 
     combined = in_parts(ws[...].astype(F32) * scale, w1[2 * chan : (rows + 4) * chan, :])
-    left = [recv[pl.ds(5 + p, count, stride=14), :] for p in range(share)]
+    left = [got[pl.ds(15 + p, count, stride=LAST), :] for p in range(share)]
     taps = TAPS // 2
     whole = [jnp.concatenate([v[:, h * chan : (h + 1) * chan] for v in left], axis=0)[:taps] for h in range(2)]
     whole = jnp.concatenate(whole, axis=0)
@@ -1060,7 +1060,7 @@
         edge_masks,
     )
     recv = exchange(payload)
-    grad, kept_half, sent_half, totals, stats_two = run(
+    grad, kept_half, sent_half, totals, stats_two, row_pairs = run(
         backward_scaled,
         [
             kept((rows * chan, frame_dev)),
@@ -1068,6 +1068,7 @@
             kept((TAPS // 2 + devices, 128)),
             kept((8, 128)),
             kept((chan + 8, 128)),
+            kept((rows // 2 * chan, frame_dev)),
         ],
         [
             pltpu.VMEM((rows // 2 * chan, frame_dev), F32),
@@ -1082,9 +1083,9 @@
         masks,
     )
     received = lax.ppermute(sent_half, "tm", [(i, i ^ 1) for i in range(n_tm)])
-    pre_ring, ring, rim, row_pairs = run(
+    pre_ring, ring, rim = run(
         around,
-        [kept((4 * chan, wide)), kept((4 * chan, wide)), kept((rows * chan, RIM)), kept((rows // 2 * chan, frame_dev))],
+        [kept((4 * chan, wide)), kept((4 * chan, wide)), kept((rows * chan, RIM))],
         [
             pltpu.VMEM(((rows // 2 + 2) * chan, RIM), F32),
             pltpu.VMEM((2 * chan, frame_dev), F32),
@@ -1118,7 +1119,7 @@
         [
             kept(((rows + 4) * chan, wide), BF16),
             kept((rows * chan, frame_dev), BF16),
-            kept((devices * 14, 128)),
+            kept((devices, LAST, 128), BF16),
             kept((8, 128)),
         ],
         [
@@ -1140,7 +1141,7 @@
         masks,
         wb,
     )
-    recv = exchange_rows(payload)
+    recv = exchange(payload)
     pooled, gain_two_grad, bias_two_grad = run(
         pool,
         [shape((1, chan, rows // 2, half), BF16), shape((1, chan)), shape((1, chan))],
@@ -1191,6 +1192,7 @@
             pltpu.VMEM((9, chan, chan), F32),
             pltpu.VMEM((1, chan), F32),
             pltpu.VMEM((1, chan), F32),
+            pltpu.VMEM((devices * LAST, 128), F32),
             pltpu.SemaphoreType.DMA((5,)),
         ],
         recv,

time: 61.1 us -> 60.4 us (0.989)
  no operation moved by 1% of the time
where the time goes in v3:
time: 60.4 us; the launch traced here: 60.1 us
  blocking collectives  19.5 us (32%)
  Pallas kernels  18.1 us (30%)
  waiting for transfers between devices  11.8 us (20%)
  starting transfers between devices  9.88 us (16%)
  between operations  0.7 us (1%)
    all_to_all x2, blocking collectives, exchange(): return lax.all_to_all(blocks, axes, 0, 0, tiled=True)  19.5 us
    pallas_call x10, Pallas kernels, run(): pl.pallas_call(kernel, out_shape=outs, in_specs=specs, out_specs=[pl.Bloc...  18.1 us
    all_to_all x2, waiting for transfers between devices, exchange(): return lax.all_to_all(blocks, axes, 0, 0, tiled=True)  11.8 us
    all_to_all x2, starting transfers between devices, exchange(): return lax.all_to_all(blocks, axes, 0, 0, tiled=True)  9.42 us
  transfers between devices with their start and end apart: 3, of which 2 were waited for; matrix products, arithmetic and copies ran while one was open for 0% of the time, Pallas kernels for 11%

profile of v3, /device:TPU:1, one launch (start us, length us, event | category | flops | bytes accessed | tf_op | source)
XLA Modules:
  0.0 60.1 jit_solution(1214623305283601658)
XLA Ops:
  0.6 2.0 %shard_map.152 = (bf16[32,16,128]{2,1,0:T(8,128)(2,1)}, bf16[1,64,8,128]{3,2,1,0:T(8,128)(2,1)S(1)}, bf16[1,16,256]{2,1,0:T(8,128)(2,1)S(1)}, f32[8,384]{1,0:T(8,128)S(1)}) custom-call(bf16[1,16,256]{2,1,0:T(8,128)(2,1)} %spec_hbm.1, bf16[1,64,8,128]{3,2,1,0:T(8,128)(2,1)} %grad_hbm.1, s32[1,4]{1,0:T(1,128)} %bounds_hbm.3), custom_call_target="tpu_custom_call" | custom-call | flops 100000000 | bytes 4000000 | tf_op jit(solution)/shard_map/pallas_call | solution.py:934
  2.7 7.1 %all-to-all-start = ((bf16[32,16,128]{2,1,0:T(8,128)(2,1)}), bf16[32,16,128]{2,1,0:T(8,128)(2,1)S(1)}, u32[]{:S(2)}, u32[]{:S(2)}) async-start(bf16[32,16,128]{2,1,0:T(8,128)(2,1)} %get-tuple-element.55), calls=%async_computation | async-start | bytes 262144 | tf_op jit(solution)/shard_map/all_to_all | solution.py:958
  9.8 2.1 %shard_map.153 = (bf16[128,768]{1,0:T(8,128)(2,1)S(1)}, bf16[128,768]{1,0:T(8,128)(2,1)S(1)}, bf16[1408,128]{1,0:T(8,128)(2,1)S(1)}, bf16[48,1152]{1,0:T(8,128)(...) custom-call(bf16[1,64,8,128]{3,2,1,0:T(8,128)(2,1)S(1)} %get-tuple-e, ...), custom_call_target="tpu_custom_call" | custom-call | flops 100000000 | bytes 4000000 | tf_op jit(solution)/shard_map/pallas_call | solution.py:934
  11.9 6.1 %all-to-all-done.recv = bf16[32,16,128]{2,1,0:T(8,128)(2,1)S(1)} async-done(((bf16[32,16,128]{2,1,0:T(8,128)(2,1)}), bf16[32,16,128]{2,1,0:T(8,128)(2,1)S(1)}, u32[]{:S(2)}, u32[]{:S(2)}) %all-to-all-start) | async-done | bytes 131104 | tf_op jit(solution)/shard_map/all_to_all | solution.py:958
  18.0 2.5 %shard_map.154 = (f32[1024,384]{1,0:T(8,128)S(1)}, bf16[32,8,128]{2,1,0:T(8,128)(2,1)S(1)}, bf16[4224,384]{1,0:T(8,128)(2,1)S(1)}, bf16[128,384]{1,0:T(8,128)(2,...) custom-call(bf16[32,16,128]{2,1,0:T(8,128)(2,1)S(1)} %all-to-all-done.recv, ...), custom_call_target="tpu_custom_call" | custom-call | flops 100000000 | bytes 4000000 | tf_op jit(solution)/shard_map/pallas_call | solution.py:934
  20.5 8.9 %all_to_all.20.recv = bf16[32,8,128]{2,1,0:T(8,128)(2,1)S(1)} all-to-all(bf16[32,8,128]{2,1,0:T(8,128)(2,1)S(1)} %get-tuple-element.67), channel_id=1, replica_groups=mesh['mel'=4,'tm'=8] {'mel','tm'}, dimensions={0} | all-to-all | bytes 131072 | tf_op jit(solution)/shard_map/all_to_all | solution.py:958
  29.4 2.3 %shard_map.155 = (f32[1024,256]{1,0:T(8,128)S(1)}, f32[320,128]{1,0:T(8,128)S(1)}, f32[320,128]{1,0:T(8,128)S(1)}, f32[8,128]{1,0:T(8,128)S(1)}, f32[72,128]{1,0:T(8,128)S(1)}, /*index=5*/f32[512,256]{1,0:T(8,128)S(1)}) custom-call(bf16[32,8,128]{2,1,0:T(8,128)(2,1)S(1)} %all_to_all.20.recv, f32[1024,384]{1,0:T(8,128)S(1)} %get-tuple-element.68.pre_two, ...), custom_call_target="tpu_custom_call" | custom-call | flops 100000000 | bytes 4000000 | tf_op jit(solution)/shard_map/pallas_call | solution.py:934
  31.7 0.5 collective-permute-start
  32.2 1.2 %shard_map.156 = (f32[256,384]{1,0:T(8,128)S(1)}, f32[256,384]{1,0:T(8,128)S(1)}, f32[1024,128]{1,0:T(8,128)S(1)}) custom-call(bf16[32,8,128]{2,1,0:T(8,128)(2,1)S(1)} %all_to_all.20.recv, f32[1024,384]{1,0:T(8,128)S(1)} %get-tuple-element.68.pre_two, bf16[4224,384]{1,0:T(8,128)(2,1)S(1)} %get-tuple-element.69.act, ...), custom_call_target="tpu_custom_call" | custom-call | flops 100000000 | bytes 4000000 | tf_op jit(solution)/shard_map/pallas_call | solution.py:934
  33.4 0.0 collective-permute-done.received
  33.5 10.6 %all_to_all.21 = f32[352,1,128]{2,1,0:T(1,128)S(1)} all-to-all(f32[352,1,128]{2,1,0:T(1,128)S(1)} %bitcast.21), channel_id=1, replica_groups=mesh['mel'=4,'tm'=8] {'mel','tm'}, dimensions={0} | all-to-all | bytes 360448 | tf_op jit(solution)/shard_map/all_to_all | solution.py:958
  44.1 3.1 %shard_map.158 = (bf16[1280,384]{1,0:T(8,128)(2,1)S(1)}, bf16[1024,256]{1,0:T(8,128)(2,1)S(1)}, bf16[32,24,128]{2,1,0:T(8,128)(2,1)}, f32[8,128]{1,0:T(8,128)S(1)}) custom-call(f32[352,128]{1,0:T(8,128)S(1)} %bitcast.20, f32[1024,384]{1,0:T(8,128)S(1)} %get-tuple-element.68.pre_two, f32[256,384]{1,0:T(8,128)S(1)} %get-tuple-element.79.pre_ring, ...), custom_call_target="tpu_custom_call" | custom-call | flops 100000000 | bytes 4000000 | tf_op jit(solution)/shard_map/pallas_call | solution.py:934
  47.2 2.3 %all-to-all-start.3 = ((bf16[32,24,128]{2,1,0:T(8,128)(2,1)}), bf16[32,24,128]{2,1,0:T(8,128)(2,1)S(1)}, u32[]{:S(2)}, u32[]{:S(2)}) async-start(bf16[32,24,128]{2,1,0:T(8,128)(2,1)} %get-tuple-element.86), calls=%async_computation.3 | async-start | bytes 393216 | tf_op jit(solution)/shard_map/all_to_all | solution.py:958
  49.5 1.3 %shard_map.159 = (bf16[1,64,8,128]{3,2,1,0:T(8,128)(2,1)}, f32[1,64]{1,0:T(1,128)}, f32[1,64]{1,0:T(1,128)}) custom-call(f32[8,128]{1,0:T(8,128)S(1)} %get-tuple-element.83.totals, f32[512,256]{1,0:T(8,128)S(1)} %get-tuple-element.84.pairs), custom_call_target="tpu_custom_call" | custom-call | flops 100000000 | bytes 4000000 | tf_op jit(solution)/shard_map/pallas_call | solution.py:934
  50.7 2.2 %shard_map.160 = (f32[48,384]{1,0:T(8,128)S(1)}, bf16[48,1152]{1,0:T(8,128)(2,1)S(1)}, f32[32,64]{1,0:T(8,128)S(1)}) custom-call(bf16[1280,384]{1,0:T(8,128)(2,1)S(1)} %get-tuple-element.89.grad, bf16[1024,256]{1,0:T(8,128)(2,1)S(1)} %get-tuple-element.90.own_low, bf16[1408,128]{1,0:T(8,128)(2,1)S(1)} %get-tuple-element.61.w1, ...), custom_call_target="tpu_custom_call" | custom-call | flops 100000000 | bytes 4000000 | tf_op jit(solution)/shard_map/pallas_call | solution.py:934
  52.9 5.7 %all-to-all-done.3.recv = bf16[32,24,128]{2,1,0:T(8,128)(2,1)S(1)} async-done(((bf16[32,24,128]{2,1,0:T(8,128)(2,1)}), bf16[32,24,128]{2,1,0:T(8,128)(2,1)S(1)}, u32[]{:S(2)}, u32[]{:S(2)}) %all-to-all-start.3) | async-done | bytes 196640 | tf_op jit(solution)/shard_map/all_to_all | solution.py:958
  58.6 1.5 %shard_map.161 = (f32[1,16,256]{2,1,0:T(8,128)}, f32[3,3,64]{2,1,0:T(4,128)}, f32[9,64,64]{2,1,0:T(8,128)}, f32[1,64]{1,0:T(1,128)}, f32[1,64]{1,0:T(1,128)}) custom-call(bf16[32,24,128]{2,1,0:T(8,128)(2,1)S(1)} %all-to-all-done.3.recv, f32[8,128]{1,0:T(8,128)S(1)} %get-tuple-element.87.features, f32[144,128]{1,0:T(8,128)S(1)} %get-tuple-element.76.stats_one.stats, ...), custom_call_target="tpu_custom_call" | custom-call | flops 100000000 | bytes 4000000 | tf_op jit(solution)/shard_map/pallas_call | solution.py:934
  (1 shorter events, 0.0 us)
Async XLA Ops:
  2.7 15.3 %all-to-all-start = ((bf16[32,16,128]{2,1,0:T(8,128)(2,1)}), bf16[32,16,128]{2,1,0:T(8,128)(2,1)S(1)}, u32[]{:S(2)}, u32[]{:S(2)}) async-start(bf16[32,16,128]{2,1,0:T(8,128)(2,1)} %get-tuple-element.55), calls=%async_computation | async-start | bytes 262144 | tf_op jit(solution)/shard_map/all_to_all | solution.py:958
  31.7 1.7 %collective-permute-start = (f32[320,128]{1,0:T(8,128)S(1)}, f32[320,128]{1,0:T(8,128)S(1)}, u32[]{:S(2)}, u32[]{:S(2)}) collective-permute-start(f32[320,128]{1,0:T(8,128)S(1)} %get-tuple-element.72), channel_id=1, source_target_pairs={{0,1},{1,0},{2,3},{3,2},{4,5},{5,4},{6,7},{7,6},{8,9},{9,8},{10,11... | collective-permute-start | bytes 491528 | tf_op jit(solution)/shard_map/ppermute | solution.py:1085
  47.2 11.5 %all-to-all-start.3 = ((bf16[32,24,128]{2,1,0:T(8,128)(2,1)}), bf16[32,24,128]{2,1,0:T(8,128)(2,1)S(1)}, u32[]{:S(2)}, u32[]{:S(2)}) async-start(bf16[32,24,128]{2,1,0:T(8,128)(2,1)} %get-tuple-element.86), calls=%async_computation.3 | async-start | bytes 393216 | tf_op jit(solution)/shard_map/all_to_all | solution.py:958

commit v4 on v3

--- a/solution.py
+++ b/solution.py
@@ -50,14 +50,15 @@
 
 def frame_masks(bounds, frames):
     last = bounds.shape[1] - 1
+    end = bounds[:, last:]
 
     def living(f):
-        return (f >= 0) & (f < bounds[0, last])
+        return (f >= 0) & (f < end)
 
     def paired(f):
         both = living(f) & living(f + 1)
         for k in range(1, last):
-            both = both & (f + 1 != bounds[0, k])
+            both = both & (f + 1 != bounds[:, k : k + 1])
         return both
 
     return tuple(m.astype(F32) for m in (living(frames), paired(frames - 1), paired(frames)))
@@ -105,8 +106,8 @@
     lane = iota((1, wide), 1)
     frames = lax.axis_index("tm") * frame_dev + jnp.where(lane < frame_dev + RIM // 2, lane, lane - wide)
     last = bounds.shape[1] - 1
-    pixels = (bounds[0, last] * (lax.axis_size("mel") * rows)).astype(F32)
-    found = frame_masks(bounds, frames)
+    pixels = bounds[:, last:].astype(F32) * (lax.axis_size("mel") * rows)
+    found = frame_masks(bounds[...], frames)
     masks[...] = jnp.concatenate(
         list(found) + [jnp.full((1, wide), 1.0) * pixels, jnp.zeros((4, wide), F32)], axis=0
     )
@@ -229,13 +230,13 @@
     store_ws.start()
     count, frame_dev = all_masks.shape[0] // 3, all_masks.shape[1]
     frames = iota((count, frame_dev), 0) * frame_dev + iota((count, frame_dev), 1)
-    for n, mask in enumerate(frame_masks(bounds, frames)):
+    for n, mask in enumerate(frame_masks(bounds[...], frames)):
         all_masks[n * count : (n + 1) * count] = mask
     q = iota(edge_masks.shape, 0)
     lane = iota(edge_masks.shape, 1)
     k = q % 8
     frames = (q // 8) * frame_dev + jnp.where(k < 4, k, k + frame_dev - 8)
-    living, behind, ahead = frame_masks(bounds, frames)
+    living, behind, ahead = frame_masks(bounds[...], frames)
     living = jnp.where((k == 0) | (k == 7), living, 0.0)
     edge_masks[...] = jnp.where(lane == 0, living, jnp.where(lane == 1, behind, jnp.where(lane == 2, ahead, 0.0)))
     params[...] = jnp.concatenate(
@@ -747,11 +748,8 @@
     table = jnp.zeros((chan, 128), F32)
 
     def tap_sums(m):
-        part = g1[m * chan : (m + 4) * chan, :]
-        high = lax.reduce_precision(part, 8, 7)
-        low = (part - high).astype(BF16)
-        taps_in = x3[:, :frame_dev]
-        products = dot(high.astype(BF16), taps_in, ((1,), (1,))) + dot(low, taps_in, ((1,), (1,)))
+        taps_in = jnp.concatenate([x3[:, :frame_dev]] * 2, axis=1)
+        products = dot(g1[m * chan : (m + 4) * chan, :], taps_in, ((1,), (1,)))
         moved = [pltpu.roll(products[k * chan : (k + 1) * chan], 128 - (m + k + 3), 1) for k in range(4)]
         return (moved[0] + moved[1]) + (moved[2] + moved[3])
 
@@ -782,7 +780,8 @@
             _, slope = silu_halves(pre_one[at, :] * scale + shift)
             value = result[n * chan : (n + 1) * chan] * slope * own_mask
             own_low[at, :] = (value * factor_one).astype(BF16)
-            g1[at, :] = value
+            g1[at, :frame_dev] = value.astype(BF16)
+            g1[at, frame_dev:] = (value - g1[at, :frame_dev].astype(F32)).astype(BF16)
         if start % 4 == 2 and start > 2:
             table = table + tap_sums(start - 6)
     table = table + tap_sums(rows - 4)
@@ -980,7 +979,7 @@
             kept((8, wide)),
         ],
         [
-            pltpu.SMEM(clip_bounds.shape, jnp.int32),
+            pltpu.VMEM(clip_bounds.shape, jnp.int32),
             pltpu.VMEM((2 * chan, half), F32),
             pltpu.VMEM((devices * FIRST, 128), F32),
             pltpu.SemaphoreType.DMA((3,)),
@@ -1013,7 +1012,7 @@
             pltpu.VMEM((9, chan, chan), BF16),
             pltpu.VMEM((3, 3, chan), BF16),
             pltpu.VMEM((4, 1, chan), F32),
-            pltpu.SMEM(clip_bounds.shape, jnp.int32),
+            pltpu.VMEM(clip_bounds.shape, jnp.int32),
             pltpu.VMEM((rows * 3, (rows + 2) * chan), BF16),
             pltpu.VMEM((chan * rows // 2, half), F32),
             pltpu.SemaphoreType.DMA((8,)),
@@ -1125,7 +1124,7 @@
         [
             pltpu.VMEM(((rows + 2) * 3 * chan, frame_dev), BF16),
             pltpu.VMEM((rows * chan, frame_dev), F32),
-            pltpu.VMEM((rows * chan, frame_dev), F32),
+            pltpu.VMEM((rows * chan, 2 * frame_dev), BF16),
         ],
         recv,
         pre_two,

time: 60.4 us -> 60.3 us (level)
  no operation moved by 1% of the time
where the time goes in v4:
time: 60.3 us; the launch traced here: 59.9 us
  blocking collectives  19.5 us (32%)
  Pallas kernels  17.9 us (30%)
  waiting for transfers between devices  11.9 us (20%)
  starting transfers between devices  9.88 us (16%)
  between operations  0.7 us (1%)
    all_to_all x2, blocking collectives, exchange(): return lax.all_to_all(blocks, axes, 0, 0, tiled=True)  19.5 us
    pallas_call x10, Pallas kernels, run(): pl.pallas_call(kernel, out_shape=outs, in_specs=specs, out_specs=[pl.Bloc...  17.9 us
    all_to_all x2, waiting for transfers between devices, exchange(): return lax.all_to_all(blocks, axes, 0, 0, tiled=True)  11.9 us
    all_to_all x2, starting transfers between devices, exchange(): return lax.all_to_all(blocks, axes, 0, 0, tiled=True)  9.42 us
  transfers between devices with their start and end apart: 3, of which 2 were waited for; matrix products, arithmetic and copies ran while one was open for 0% of the time, Pallas kernels for 11%

profile of v4, /device:TPU:1, one launch (start us, length us, event | category | flops | bytes accessed | tf_op | source)
XLA Modules:
  0.0 59.9 jit_solution(418859687196681985)
XLA Ops:
  0.6 2.1 %shard_map.152 = (bf16[32,16,128]{2,1,0:T(8,128)(2,1)}, bf16[1,64,8,128]{3,2,1,0:T(8,128)(2,1)S(1)}, bf16[1,16,256]{2,1,0:T(8,128)(2,1)S(1)}, f32[8,384]{1,0:T(8,128)S(1)}) custom-call(bf16[1,16,256]{2,1,0:T(8,128)(2,1)} %spec_hbm.1, bf16[1,64,8,128]{3,2,1,0:T(8,128)(2,1)} %grad_hbm.1, s32[1,4]{1,0:T(1,128)} %bounds_hbm.3), custom_call_target="tpu_custom_call" | custom-call | flops 100000000 | bytes 4000000 | tf_op jit(solution)/shard_map/pallas_call | solution.py:933
  2.7 7.1 %all-to-all-start = ((bf16[32,16,128]{2,1,0:T(8,128)(2,1)}), bf16[32,16,128]{2,1,0:T(8,128)(2,1)S(1)}, u32[]{:S(2)}, u32[]{:S(2)}) async-start(bf16[32,16,128]{2,1,0:T(8,128)(2,1)} %get-tuple-element.55), calls=%async_computation | async-start | bytes 262144 | tf_op jit(solution)/shard_map/all_to_all | solution.py:957
  9.8 2.0 %shard_map.153 = (bf16[128,768]{1,0:T(8,128)(2,1)S(1)}, bf16[128,768]{1,0:T(8,128)(2,1)S(1)}, bf16[1408,128]{1,0:T(8,128)(2,1)S(1)}, bf16[48,1152]{1,0:T(8,128)(...) custom-call(bf16[1,64,8,128]{3,2,1,0:T(8,128)(2,1)S(1)} %get-tuple-e, ...), custom_call_target="tpu_custom_call" | custom-call | flops 100000000 | bytes 4000000 | tf_op jit(solution)/shard_map/pallas_call | solution.py:933
  11.8 6.2 %all-to-all-done.recv = bf16[32,16,128]{2,1,0:T(8,128)(2,1)S(1)} async-done(((bf16[32,16,128]{2,1,0:T(8,128)(2,1)}), bf16[32,16,128]{2,1,0:T(8,128)(2,1)S(1)}, u32[]{:S(2)}, u32[]{:S(2)}) %all-to-all-start) | async-done | bytes 131104 | tf_op jit(solution)/shard_map/all_to_all | solution.py:957
  18.1 2.5 %shard_map.154 = (f32[1024,384]{1,0:T(8,128)S(1)}, bf16[32,8,128]{2,1,0:T(8,128)(2,1)S(1)}, bf16[4224,384]{1,0:T(8,128)(2,1)S(1)}, bf16[128,384]{1,0:T(8,128)(2,...) custom-call(bf16[32,16,128]{2,1,0:T(8,128)(2,1)S(1)} %all-to-all-done.recv, ...), custom_call_target="tpu_custom_call" | custom-call | flops 100000000 | bytes 4000000 | tf_op jit(solution)/shard_map/pallas_call | solution.py:933
  20.6 8.9 %all_to_all.20.recv = bf16[32,8,128]{2,1,0:T(8,128)(2,1)S(1)} all-to-all(bf16[32,8,128]{2,1,0:T(8,128)(2,1)S(1)} %get-tuple-element.67), channel_id=1, replica_groups=mesh['mel'=4,'tm'=8] {'mel','tm'}, dimensions={0} | all-to-all | bytes 131072 | tf_op jit(solution)/shard_map/all_to_all | solution.py:957
  29.5 2.3 %shard_map.155 = (f32[1024,256]{1,0:T(8,128)S(1)}, f32[320,128]{1,0:T(8,128)S(1)}, f32[320,128]{1,0:T(8,128)S(1)}, f32[8,128]{1,0:T(8,128)S(1)}, f32[72,128]{1,0:T(8,128)S(1)}, /*index=5*/f32[512,256]{1,0:T(8,128)S(1)}) custom-call(bf16[32,8,128]{2,1,0:T(8,128)(2,1)S(1)} %all_to_all.20.recv, f32[1024,384]{1,0:T(8,128)S(1)} %get-tuple-element.68.pre_two, ...), custom_call_target="tpu_custom_call" | custom-call | flops 100000000 | bytes 4000000 | tf_op jit(solution)/shard_map/pallas_call | solution.py:933
  31.8 0.5 collective-permute-start
  32.2 1.2 %shard_map.156 = (f32[256,384]{1,0:T(8,128)S(1)}, f32[256,384]{1,0:T(8,128)S(1)}, f32[1024,128]{1,0:T(8,128)S(1)}) custom-call(bf16[32,8,128]{2,1,0:T(8,128)(2,1)S(1)} %all_to_all.20.recv, f32[1024,384]{1,0:T(8,128)S(1)} %get-tuple-element.68.pre_two, bf16[4224,384]{1,0:T(8,128)(2,1)S(1)} %get-tuple-element.69.act, ...), custom_call_target="tpu_custom_call" | custom-call | flops 100000000 | bytes 4000000 | tf_op jit(solution)/shard_map/pallas_call | solution.py:933
  33.5 0.0 collective-permute-done.received
  33.5 10.6 %all_to_all.21 = f32[352,1,128]{2,1,0:T(1,128)S(1)} all-to-all(f32[352,1,128]{2,1,0:T(1,128)S(1)} %bitcast.21), channel_id=1, replica_groups=mesh['mel'=4,'tm'=8] {'mel','tm'}, dimensions={0} | all-to-all | bytes 360448 | tf_op jit(solution)/shard_map/all_to_all | solution.py:957
  44.1 2.9 %shard_map.158 = (bf16[1280,384]{1,0:T(8,128)(2,1)S(1)}, bf16[1024,256]{1,0:T(8,128)(2,1)S(1)}, bf16[32,24,128]{2,1,0:T(8,128)(2,1)}, f32[8,128]{1,0:T(8,128)S(1)}) custom-call(f32[352,128]{1,0:T(8,128)S(1)} %bitcast.20, f32[1024,384]{1,0:T(8,128)S(1)} %get-tuple-element.68.pre_two, f32[256,384]{1,0:T(8,128)S(1)} %get-tuple-element.79.pre_ring, ...), custom_call_target="tpu_custom_call" | custom-call | flops 100000000 | bytes 4000000 | tf_op jit(solution)/shard_map/pallas_call | solution.py:933
  47.0 2.3 %all-to-all-start.3 = ((bf16[32,24,128]{2,1,0:T(8,128)(2,1)}), bf16[32,24,128]{2,1,0:T(8,128)(2,1)S(1)}, u32[]{:S(2)}, u32[]{:S(2)}) async-start(bf16[32,24,128]{2,1,0:T(8,128)(2,1)} %get-tuple-element.86), calls=%async_computation.3 | async-start | bytes 393216 | tf_op jit(solution)/shard_map/all_to_all | solution.py:957
  49.3 1.3 %shard_map.159 = (bf16[1,64,8,128]{3,2,1,0:T(8,128)(2,1)}, f32[1,64]{1,0:T(1,128)}, f32[1,64]{1,0:T(1,128)}) custom-call(f32[8,128]{1,0:T(8,128)S(1)} %get-tuple-element.83.totals, f32[512,256]{1,0:T(8,128)S(1)} %get-tuple-element.84.pairs), custom_call_target="tpu_custom_call" | custom-call | flops 100000000 | bytes 4000000 | tf_op jit(solution)/shard_map/pallas_call | solution.py:933
  50.6 2.2 %shard_map.160 = (f32[48,384]{1,0:T(8,128)S(1)}, bf16[48,1152]{1,0:T(8,128)(2,1)S(1)}, f32[32,64]{1,0:T(8,128)S(1)}) custom-call(bf16[1280,384]{1,0:T(8,128)(2,1)S(1)} %get-tuple-element.89.grad, bf16[1024,256]{1,0:T(8,128)(2,1)S(1)} %get-tuple-element.90.own_low, bf16[1408,128]{1,0:T(8,128)(2,1)S(1)} %get-tuple-element.61.w1, ...), custom_call_target="tpu_custom_call" | custom-call | flops 100000000 | bytes 4000000 | tf_op jit(solution)/shard_map/pallas_call | solution.py:933
  52.8 5.7 %all-to-all-done.3.recv = bf16[32,24,128]{2,1,0:T(8,128)(2,1)S(1)} async-done(((bf16[32,24,128]{2,1,0:T(8,128)(2,1)}), bf16[32,24,128]{2,1,0:T(8,128)(2,1)S(1)}, u32[]{:S(2)}, u32[]{:S(2)}) %all-to-all-start.3) | async-done | bytes 196640 | tf_op jit(solution)/shard_map/all_to_all | solution.py:957
  58.5 1.5 %shard_map.161 = (f32[1,16,256]{2,1,0:T(8,128)}, f32[3,3,64]{2,1,0:T(4,128)}, f32[9,64,64]{2,1,0:T(8,128)}, f32[1,64]{1,0:T(1,128)}, f32[1,64]{1,0:T(1,128)}) custom-call(bf16[32,24,128]{2,1,0:T(8,128)(2,1)S(1)} %all-to-all-done.3.recv, f32[8,128]{1,0:T(8,128)S(1)} %get-tuple-element.87.features, f32[144,128]{1,0:T(8,128)S(1)} %get-tuple-element.76.stats_one.stats, ...), custom_call_target="tpu_custom_call" | custom-call | flops 100000000 | bytes 4000000 | tf_op jit(solution)/shard_map/pallas_call | solution.py:933
  (1 shorter events, 0.0 us)
Async XLA Ops:
  2.7 15.3 %all-to-all-start = ((bf16[32,16,128]{2,1,0:T(8,128)(2,1)}), bf16[32,16,128]{2,1,0:T(8,128)(2,1)S(1)}, u32[]{:S(2)}, u32[]{:S(2)}) async-start(bf16[32,16,128]{2,1,0:T(8,128)(2,1)} %get-tuple-element.55), calls=%async_computation | async-start | bytes 262144 | tf_op jit(solution)/shard_map/all_to_all | solution.py:957
  31.8 1.7 %collective-permute-start = (f32[320,128]{1,0:T(8,128)S(1)}, f32[320,128]{1,0:T(8,128)S(1)}, u32[]{:S(2)}, u32[]{:S(2)}) collective-permute-start(f32[320,128]{1,0:T(8,128)S(1)} %get-tuple-element.72), channel_id=1, source_target_pairs={{0,1},{1,0},{2,3},{3,2},{4,5},{5,4},{6,7},{7,6},{8,9},{9,8},{10,11... | collective-permute-start | bytes 491528 | tf_op jit(solution)/shard_map/ppermute | solution.py:1084
  47.0 11.5 %all-to-all-start.3 = ((bf16[32,24,128]{2,1,0:T(8,128)(2,1)}), bf16[32,24,128]{2,1,0:T(8,128)(2,1)S(1)}, u32[]{:S(2)}, u32[]{:S(2)}) async-start(bf16[32,24,128]{2,1,0:T(8,128)(2,1)} %get-tuple-element.86), calls=%async_computation.3 | async-start | bytes 393216 | tf_op jit(solution)/shard_map/all_to_all | solution.py:957

commit v5 on v4

--- a/solution.py
+++ b/solution.py
@@ -113,6 +113,7 @@
     )
     usable, behind, ahead = (m[:, :frame_dev] for m in found)
     copies[1].wait()
+    copies[2].wait()
     x = spec[0].astype(F32) * usable
     lane = iota((1, frame_dev), 1)
     row = iota((rows, 1), 0)
@@ -143,7 +144,6 @@
     for d in range(devices):
         rows_out[FIRST * d : FIRST * d + 8, :] = near
     put(COLUMNS, strip)
-    copies[2].wait()
     _, chan, many, half = own.shape
     share = share_of(devices, chan)
     holders = chan // share

time: 60.3 us -> 60.2 us (level)
  no operation moved by 1% of the time
where the time goes in v5:
time: 60.2 us; the launch traced here: 59.9 us
  blocking collectives  19.5 us (32%)
  Pallas kernels  17.9 us (30%)
  waiting for transfers between devices  11.9 us (20%)
  starting transfers between devices  9.87 us (16%)
  between operations  0.7 us (1%)
    all_to_all x2, blocking collectives, exchange(): return lax.all_to_all(blocks, axes, 0, 0, tiled=True)  19.5 us
    pallas_call x10, Pallas kernels, run(): pl.pallas_call(kernel, out_shape=outs, in_specs=specs, out_specs=[pl.Bloc...  17.9 us
    all_to_all x2, waiting for transfers between devices, exchange(): return lax.all_to_all(blocks, axes, 0, 0, tiled=True)  11.9 us
    all_to_all x2, starting transfers between devices, exchange(): return lax.all_to_all(blocks, axes, 0, 0, tiled=True)  9.42 us
  transfers between devices with their start and end apart: 3, of which 2 were waited for; matrix products, arithmetic and copies ran while one was open for 0% of the time, Pallas kernels for 11%

profile of v5, /device:TPU:1, one launch (start us, length us, event | category | flops | bytes accessed | tf_op | source)
XLA Modules:
  0.0 59.9 jit_solution(12711253193473389502)
XLA Ops:
  0.6 2.0 %shard_map.152 = (bf16[32,16,128]{2,1,0:T(8,128)(2,1)}, bf16[1,64,8,128]{3,2,1,0:T(8,128)(2,1)S(1)}, bf16[1,16,256]{2,1,0:T(8,128)(2,1)S(1)}, f32[8,384]{1,0:T(8,128)S(1)}) custom-call(bf16[1,16,256]{2,1,0:T(8,128)(2,1)} %spec_hbm.1, bf16[1,64,8,128]{3,2,1,0:T(8,128)(2,1)} %grad_hbm.1, s32[1,4]{1,0:T(1,128)} %bounds_hbm.3), custom_call_target="tpu_custom_call" | custom-call | flops 100000000 | bytes 4000000 | tf_op jit(solution)/shard_map/pallas_call | solution.py:933
  2.7 7.1 %all-to-all-start = ((bf16[32,16,128]{2,1,0:T(8,128)(2,1)}), bf16[32,16,128]{2,1,0:T(8,128)(2,1)S(1)}, u32[]{:S(2)}, u32[]{:S(2)}) async-start(bf16[32,16,128]{2,1,0:T(8,128)(2,1)} %get-tuple-element.55), calls=%async_computation | async-start | bytes 262144 | tf_op jit(solution)/shard_map/all_to_all | solution.py:957
  9.8 2.0 %shard_map.153 = (bf16[128,768]{1,0:T(8,128)(2,1)S(1)}, bf16[128,768]{1,0:T(8,128)(2,1)S(1)}, bf16[1408,128]{1,0:T(8,128)(2,1)S(1)}, bf16[48,1152]{1,0:T(8,128)(...) custom-call(bf16[1,64,8,128]{3,2,1,0:T(8,128)(2,1)S(1)} %get-tuple-e, ...), custom_call_target="tpu_custom_call" | custom-call | flops 100000000 | bytes 4000000 | tf_op jit(solution)/shard_map/pallas_call | solution.py:933
  11.8 6.2 %all-to-all-done.recv = bf16[32,16,128]{2,1,0:T(8,128)(2,1)S(1)} async-done(((bf16[32,16,128]{2,1,0:T(8,128)(2,1)}), bf16[32,16,128]{2,1,0:T(8,128)(2,1)S(1)}, u32[]{:S(2)}, u32[]{:S(2)}) %all-to-all-start) | async-done | bytes 131104 | tf_op jit(solution)/shard_map/all_to_all | solution.py:957
  18.0 2.5 %shard_map.154 = (f32[1024,384]{1,0:T(8,128)S(1)}, bf16[32,8,128]{2,1,0:T(8,128)(2,1)S(1)}, bf16[4224,384]{1,0:T(8,128)(2,1)S(1)}, bf16[128,384]{1,0:T(8,128)(2,...) custom-call(bf16[32,16,128]{2,1,0:T(8,128)(2,1)S(1)} %all-to-all-done.recv, ...), custom_call_target="tpu_custom_call" | custom-call | flops 100000000 | bytes 4000000 | tf_op jit(solution)/shard_map/pallas_call | solution.py:933
  20.5 8.9 %all_to_all.20.recv = bf16[32,8,128]{2,1,0:T(8,128)(2,1)S(1)} all-to-all(bf16[32,8,128]{2,1,0:T(8,128)(2,1)S(1)} %get-tuple-element.67), channel_id=1, replica_groups=mesh['mel'=4,'tm'=8] {'mel','tm'}, dimensions={0} | all-to-all | bytes 131072 | tf_op jit(solution)/shard_map/all_to_all | solution.py:957
  29.4 2.3 %shard_map.155 = (f32[1024,256]{1,0:T(8,128)S(1)}, f32[320,128]{1,0:T(8,128)S(1)}, f32[320,128]{1,0:T(8,128)S(1)}, f32[8,128]{1,0:T(8,128)S(1)}, f32[72,128]{1,0:T(8,128)S(1)}, /*index=5*/f32[512,256]{1,0:T(8,128)S(1)}) custom-call(bf16[32,8,128]{2,1,0:T(8,128)(2,1)S(1)} %all_to_all.20.recv, f32[1024,384]{1,0:T(8,128)S(1)} %get-tuple-element.68.pre_two, ...), custom_call_target="tpu_custom_call" | custom-call | flops 100000000 | bytes 4000000 | tf_op jit(solution)/shard_map/pallas_call | solution.py:933
  31.8 0.4 collective-permute-start
  32.2 1.2 %shard_map.156 = (f32[256,384]{1,0:T(8,128)S(1)}, f32[256,384]{1,0:T(8,128)S(1)}, f32[1024,128]{1,0:T(8,128)S(1)}) custom-call(bf16[32,8,128]{2,1,0:T(8,128)(2,1)S(1)} %all_to_all.20.recv, f32[1024,384]{1,0:T(8,128)S(1)} %get-tuple-element.68.pre_two, bf16[4224,384]{1,0:T(8,128)(2,1)S(1)} %get-tuple-element.69.act, ...), custom_call_target="tpu_custom_call" | custom-call | flops 100000000 | bytes 4000000 | tf_op jit(solution)/shard_map/pallas_call | solution.py:933
  33.4 0.0 collective-permute-done.received
  33.5 10.6 %all_to_all.21 = f32[352,1,128]{2,1,0:T(1,128)S(1)} all-to-all(f32[352,1,128]{2,1,0:T(1,128)S(1)} %bitcast.21), channel_id=1, replica_groups=mesh['mel'=4,'tm'=8] {'mel','tm'}, dimensions={0} | all-to-all | bytes 360448 | tf_op jit(solution)/shard_map/all_to_all | solution.py:957
  44.1 2.9 %shard_map.158 = (bf16[1280,384]{1,0:T(8,128)(2,1)S(1)}, bf16[1024,256]{1,0:T(8,128)(2,1)S(1)}, bf16[32,24,128]{2,1,0:T(8,128)(2,1)}, f32[8,128]{1,0:T(8,128)S(1)}) custom-call(f32[352,128]{1,0:T(8,128)S(1)} %bitcast.20, f32[1024,384]{1,0:T(8,128)S(1)} %get-tuple-element.68.pre_two, f32[256,384]{1,0:T(8,128)S(1)} %get-tuple-element.79.pre_ring, ...), custom_call_target="tpu_custom_call" | custom-call | flops 100000000 | bytes 4000000 | tf_op jit(solution)/shard_map/pallas_call | solution.py:933
  47.0 2.3 %all-to-all-start.3 = ((bf16[32,24,128]{2,1,0:T(8,128)(2,1)}), bf16[32,24,128]{2,1,0:T(8,128)(2,1)S(1)}, u32[]{:S(2)}, u32[]{:S(2)}) async-start(bf16[32,24,128]{2,1,0:T(8,128)(2,1)} %get-tuple-element.86), calls=%async_computation.3 | async-start | bytes 393216 | tf_op jit(solution)/shard_map/all_to_all | solution.py:957
  49.3 1.3 %shard_map.159 = (bf16[1,64,8,128]{3,2,1,0:T(8,128)(2,1)}, f32[1,64]{1,0:T(1,128)}, f32[1,64]{1,0:T(1,128)}) custom-call(f32[8,128]{1,0:T(8,128)S(1)} %get-tuple-element.83.totals, f32[512,256]{1,0:T(8,128)S(1)} %get-tuple-element.84.pairs), custom_call_target="tpu_custom_call" | custom-call | flops 100000000 | bytes 4000000 | tf_op jit(solution)/shard_map/pallas_call | solution.py:933
  50.6 2.2 %shard_map.160 = (f32[48,384]{1,0:T(8,128)S(1)}, bf16[48,1152]{1,0:T(8,128)(2,1)S(1)}, f32[32,64]{1,0:T(8,128)S(1)}) custom-call(bf16[1280,384]{1,0:T(8,128)(2,1)S(1)} %get-tuple-element.89.grad, bf16[1024,256]{1,0:T(8,128)(2,1)S(1)} %get-tuple-element.90.own_low, bf16[1408,128]{1,0:T(8,128)(2,1)S(1)} %get-tuple-element.61.w1, ...), custom_call_target="tpu_custom_call" | custom-call | flops 100000000 | bytes 4000000 | tf_op jit(solution)/shard_map/pallas_call | solution.py:933
  52.8 5.7 %all-to-all-done.3.recv = bf16[32,24,128]{2,1,0:T(8,128)(2,1)S(1)} async-done(((bf16[32,24,128]{2,1,0:T(8,128)(2,1)}), bf16[32,24,128]{2,1,0:T(8,128)(2,1)S(1)}, u32[]{:S(2)}, u32[]{:S(2)}) %all-to-all-start.3) | async-done | bytes 196640 | tf_op jit(solution)/shard_map/all_to_all | solution.py:957
  58.5 1.5 %shard_map.161 = (f32[1,16,256]{2,1,0:T(8,128)}, f32[3,3,64]{2,1,0:T(4,128)}, f32[9,64,64]{2,1,0:T(8,128)}, f32[1,64]{1,0:T(1,128)}, f32[1,64]{1,0:T(1,128)}) custom-call(bf16[32,24,128]{2,1,0:T(8,128)(2,1)S(1)} %all-to-all-done.3.recv, f32[8,128]{1,0:T(8,128)S(1)} %get-tuple-element.87.features, f32[144,128]{1,0:T(8,128)S(1)} %get-tuple-element.76.stats_one.stats, ...), custom_call_target="tpu_custom_call" | custom-call | flops 100000000 | bytes 4000000 | tf_op jit(solution)/shard_map/pallas_call | solution.py:933
  (1 shorter events, 0.0 us)
Async XLA Ops:
  2.7 15.3 %all-to-all-start = ((bf16[32,16,128]{2,1,0:T(8,128)(2,1)}), bf16[32,16,128]{2,1,0:T(8,128)(2,1)S(1)}, u32[]{:S(2)}, u32[]{:S(2)}) async-start(bf16[32,16,128]{2,1,0:T(8,128)(2,1)} %get-tuple-element.55), calls=%async_computation | async-start | bytes 262144 | tf_op jit(solution)/shard_map/all_to_all | solution.py:957
  31.8 1.7 %collective-permute-start = (f32[320,128]{1,0:T(8,128)S(1)}, f32[320,128]{1,0:T(8,128)S(1)}, u32[]{:S(2)}, u32[]{:S(2)}) collective-permute-start(f32[320,128]{1,0:T(8,128)S(1)} %get-tuple-element.72), channel_id=1, source_target_pairs={{0,1},{1,0},{2,3},{3,2},{4,5},{5,4},{6,7},{7,6},{8,9},{9,8},{10,11... | collective-permute-start | bytes 491528 | tf_op jit(solution)/shard_map/ppermute | solution.py:1084
  47.0 11.5 %all-to-all-start.3 = ((bf16[32,24,128]{2,1,0:T(8,128)(2,1)}), bf16[32,24,128]{2,1,0:T(8,128)(2,1)S(1)}, u32[]{:S(2)}, u32[]{:S(2)}) async-start(bf16[32,24,128]{2,1,0:T(8,128)(2,1)} %get-tuple-element.86), calls=%async_computation.3 | async-start | bytes 393216 | tf_op jit(solution)/shard_map/all_to_all | solution.py:957

commit v6 on v5

--- a/solution.py
+++ b/solution.py
@@ -297,6 +297,13 @@
             result = result + total[n * block : (n + 1) * block]
         results.append(result)
     return results if by > 1 else results[0]
+
+
+def added(ref, start, stop):
+    parts = [ref[d, start:stop].astype(F32) for d in range(ref.shape[0])]
+    while len(parts) > 1:
+        parts = [a + b for a, b in zip(parts[0::2], parts[1::2])]
+    return parts[0]
 
 
 def moved_rows(v, step):
@@ -531,10 +538,7 @@
     up[...] = dot(own_rows[...], spreading(half))
     usable = masks[0:1, :frame_dev]
     total = masks[3:4, 0:1]
-    sums = [recv[d].astype(F32) for d in range(devices)]
-    while len(sums) > 1:
-        sums = [a + b for a, b in zip(sums[0::2], sums[1::2])]
-    sums = jnp.sum(sums[0][0:3], axis=0, keepdims=True)
+    sums = jnp.sum(added(recv, 0, SECOND)[0:3], axis=0, keepdims=True)
     mean = to_column(sums, chan) / total
     inv = lax.rsqrt(to_column(sums, chan, chan) / total - mean * mean + 1e-05)
     scale = 0.5 * to_column(params[2:3], chan) * inv
@@ -866,8 +870,7 @@
     gain = params[0:1]
     count = recv.shape[0]
     share = half_share(count, 9 * chan)
-    got[...] = recv[...].astype(F32).reshape(count * LAST, 128)
-    sums = summed_blocks(got, count)
+    sums = added(recv, 0, 16)
     sums = sums[0:5] + sums[5:10] + sums[10:15]
     ten = jnp.concatenate([sums[:, :chan], sums[:, chan:]], axis=0)
     bias_sum = ten[9:10]
@@ -890,6 +893,7 @@
         return v[:many] + v[many:]
 
     combined = in_parts(ws[...].astype(F32) * scale, w1[2 * chan : (rows + 4) * chan, :])
+    got[...] = recv[...].astype(F32).reshape(count * LAST, 128)
     left = [got[pl.ds(15 + p, count, stride=LAST), :] for p in range(share)]
     taps = TAPS // 2
     whole = [jnp.concatenate([v[:, h * chan : (h + 1) * chan] for v in left], axis=0)[:taps] for h in range(2)]

time: 60.2 us -> 60.2 us (level)
  no operation moved by 1% of the time
where the time goes in v6:
time: 60.2 us; the launch traced here: 59.9 us
  blocking collectives  19.5 us (32%)
  Pallas kernels  17.9 us (30%)
  waiting for transfers between devices  11.9 us (20%)
  starting transfers between devices  9.87 us (16%)
  between operations  0.7 us (1%)
    all_to_all x2, blocking collectives, exchange(): return lax.all_to_all(blocks, axes, 0, 0, tiled=True)  19.5 us
    pallas_call x10, Pallas kernels, run(): pl.pallas_call(kernel, out_shape=outs, in_specs=specs, out_specs=[pl.Bloc...  17.9 us
    all_to_all x2, waiting for transfers between devices, exchange(): return lax.all_to_all(blocks, axes, 0, 0, tiled=True)  11.9 us
    all_to_all x2, starting transfers between devices, exchange(): return lax.all_to_all(blocks, axes, 0, 0, tiled=True)  9.42 us
  transfers between devices with their start and end apart: 3, of which 2 were waited for; matrix products, arithmetic and copies ran while one was open for 0% of the time, Pallas kernels for 11%

profile of v6, /device:TPU:1, one launch (start us, length us, event | category | flops | bytes accessed | tf_op | source)
XLA Modules:
  0.0 59.9 jit_solution(2525459251098444547)
XLA Ops:
  0.6 2.0 %shard_map.152 = (bf16[32,16,128]{2,1,0:T(8,128)(2,1)}, bf16[1,64,8,128]{3,2,1,0:T(8,128)(2,1)S(1)}, bf16[1,16,256]{2,1,0:T(8,128)(2,1)S(1)}, f32[8,384]{1,0:T(8,128)S(1)}) custom-call(bf16[1,16,256]{2,1,0:T(8,128)(2,1)} %spec_hbm.1, bf16[1,64,8,128]{3,2,1,0:T(8,128)(2,1)} %grad_hbm.1, s32[1,4]{1,0:T(1,128)} %bounds_hbm.3), custom_call_target="tpu_custom_call" | custom-call | flops 100000000 | bytes 4000000 | tf_op jit(solution)/shard_map/pallas_call | solution.py:937
  2.7 7.1 %all-to-all-start = ((bf16[32,16,128]{2,1,0:T(8,128)(2,1)}), bf16[32,16,128]{2,1,0:T(8,128)(2,1)S(1)}, u32[]{:S(2)}, u32[]{:S(2)}) async-start(bf16[32,16,128]{2,1,0:T(8,128)(2,1)} %get-tuple-element.55), calls=%async_computation | async-start | bytes 262144 | tf_op jit(solution)/shard_map/all_to_all | solution.py:961
  9.8 2.0 %shard_map.153 = (bf16[128,768]{1,0:T(8,128)(2,1)S(1)}, bf16[128,768]{1,0:T(8,128)(2,1)S(1)}, bf16[1408,128]{1,0:T(8,128)(2,1)S(1)}, bf16[48,1152]{1,0:T(8,128)(...) custom-call(bf16[1,64,8,128]{3,2,1,0:T(8,128)(2,1)S(1)} %get-tuple-e, ...), custom_call_target="tpu_custom_call" | custom-call | flops 100000000 | bytes 4000000 | tf_op jit(solution)/shard_map/pallas_call | solution.py:937
  11.8 6.2 %all-to-all-done.recv = bf16[32,16,128]{2,1,0:T(8,128)(2,1)S(1)} async-done(((bf16[32,16,128]{2,1,0:T(8,128)(2,1)}), bf16[32,16,128]{2,1,0:T(8,128)(2,1)S(1)}, u32[]{:S(2)}, u32[]{:S(2)}) %all-to-all-start) | async-done | bytes 131104 | tf_op jit(solution)/shard_map/all_to_all | solution.py:961
  18.0 2.5 %shard_map.154 = (f32[1024,384]{1,0:T(8,128)S(1)}, bf16[32,8,128]{2,1,0:T(8,128)(2,1)S(1)}, bf16[4224,384]{1,0:T(8,128)(2,1)S(1)}, bf16[128,384]{1,0:T(8,128)(2,...) custom-call(bf16[32,16,128]{2,1,0:T(8,128)(2,1)S(1)} %all-to-all-done.recv, ...), custom_call_target="tpu_custom_call" | custom-call | flops 100000000 | bytes 4000000 | tf_op jit(solution)/shard_map/pallas_call | solution.py:937
  20.5 8.9 %all_to_all.20.recv = bf16[32,8,128]{2,1,0:T(8,128)(2,1)S(1)} all-to-all(bf16[32,8,128]{2,1,0:T(8,128)(2,1)S(1)} %get-tuple-element.67), channel_id=1, replica_groups=mesh['mel'=4,'tm'=8] {'mel','tm'}, dimensions={0} | all-to-all | bytes 131072 | tf_op jit(solution)/shard_map/all_to_all | solution.py:961
  29.4 2.3 %shard_map.155 = (f32[1024,256]{1,0:T(8,128)S(1)}, f32[320,128]{1,0:T(8,128)S(1)}, f32[320,128]{1,0:T(8,128)S(1)}, f32[8,128]{1,0:T(8,128)S(1)}, f32[72,128]{1,0:T(8,128)S(1)}, /*index=5*/f32[512,256]{1,0:T(8,128)S(1)}) custom-call(bf16[32,8,128]{2,1,0:T(8,128)(2,1)S(1)} %all_to_all.20.recv, f32[1024,384]{1,0:T(8,128)S(1)} %get-tuple-element.68.pre_two, ...), custom_call_target="tpu_custom_call" | custom-call | flops 100000000 | bytes 4000000 | tf_op jit(solution)/shard_map/pallas_call | solution.py:937
  31.8 0.4 collective-permute-start
  32.2 1.2 %shard_map.156 = (f32[256,384]{1,0:T(8,128)S(1)}, f32[256,384]{1,0:T(8,128)S(1)}, f32[1024,128]{1,0:T(8,128)S(1)}) custom-call(bf16[32,8,128]{2,1,0:T(8,128)(2,1)S(1)} %all_to_all.20.recv, f32[1024,384]{1,0:T(8,128)S(1)} %get-tuple-element.68.pre_two, bf16[4224,384]{1,0:T(8,128)(2,1)S(1)} %get-tuple-element.69.act, ...), custom_call_target="tpu_custom_call" | custom-call | flops 100000000 | bytes 4000000 | tf_op jit(solution)/shard_map/pallas_call | solution.py:937
  33.4 0.0 collective-permute-done.received
  33.5 10.6 %all_to_all.21 = f32[352,1,128]{2,1,0:T(1,128)S(1)} all-to-all(f32[352,1,128]{2,1,0:T(1,128)S(1)} %bitcast.21), channel_id=1, replica_groups=mesh['mel'=4,'tm'=8] {'mel','tm'}, dimensions={0} | all-to-all | bytes 360448 | tf_op jit(solution)/shard_map/all_to_all | solution.py:961
  44.1 2.9 %shard_map.158 = (bf16[1280,384]{1,0:T(8,128)(2,1)S(1)}, bf16[1024,256]{1,0:T(8,128)(2,1)S(1)}, bf16[32,24,128]{2,1,0:T(8,128)(2,1)}, f32[8,128]{1,0:T(8,128)S(1)}) custom-call(f32[352,128]{1,0:T(8,128)S(1)} %bitcast.20, f32[1024,384]{1,0:T(8,128)S(1)} %get-tuple-element.68.pre_two, f32[256,384]{1,0:T(8,128)S(1)} %get-tuple-element.79.pre_ring, ...), custom_call_target="tpu_custom_call" | custom-call | flops 100000000 | bytes 4000000 | tf_op jit(solution)/shard_map/pallas_call | solution.py:937
  47.0 2.3 %all-to-all-start.3 = ((bf16[32,24,128]{2,1,0:T(8,128)(2,1)}), bf16[32,24,128]{2,1,0:T(8,128)(2,1)S(1)}, u32[]{:S(2)}, u32[]{:S(2)}) async-start(bf16[32,24,128]{2,1,0:T(8,128)(2,1)} %get-tuple-element.86), calls=%async_computation.3 | async-start | bytes 393216 | tf_op jit(solution)/shard_map/all_to_all | solution.py:961
  49.3 1.3 %shard_map.159 = (bf16[1,64,8,128]{3,2,1,0:T(8,128)(2,1)}, f32[1,64]{1,0:T(1,128)}, f32[1,64]{1,0:T(1,128)}) custom-call(f32[8,128]{1,0:T(8,128)S(1)} %get-tuple-element.83.totals, f32[512,256]{1,0:T(8,128)S(1)} %get-tuple-element.84.pairs), custom_call_target="tpu_custom_call" | custom-call | flops 100000000 | bytes 4000000 | tf_op jit(solution)/shard_map/pallas_call | solution.py:937
  50.6 2.2 %shard_map.160 = (f32[48,384]{1,0:T(8,128)S(1)}, bf16[48,1152]{1,0:T(8,128)(2,1)S(1)}, f32[32,64]{1,0:T(8,128)S(1)}) custom-call(bf16[1280,384]{1,0:T(8,128)(2,1)S(1)} %get-tuple-element.89.grad, bf16[1024,256]{1,0:T(8,128)(2,1)S(1)} %get-tuple-element.90.own_low, bf16[1408,128]{1,0:T(8,128)(2,1)S(1)} %get-tuple-element.61.w1, ...), custom_call_target="tpu_custom_call" | custom-call | flops 100000000 | bytes 4000000 | tf_op jit(solution)/shard_map/pallas_call | solution.py:937
  52.8 5.7 %all-to-all-done.3.recv = bf16[32,24,128]{2,1,0:T(8,128)(2,1)S(1)} async-done(((bf16[32,24,128]{2,1,0:T(8,128)(2,1)}), bf16[32,24,128]{2,1,0:T(8,128)(2,1)S(1)}, u32[]{:S(2)}, u32[]{:S(2)}) %all-to-all-start.3) | async-done | bytes 196640 | tf_op jit(solution)/shard_map/all_to_all | solution.py:961
  58.5 1.4 %shard_map.161 = (f32[1,16,256]{2,1,0:T(8,128)}, f32[3,3,64]{2,1,0:T(4,128)}, f32[9,64,64]{2,1,0:T(8,128)}, f32[1,64]{1,0:T(1,128)}, f32[1,64]{1,0:T(1,128)}) custom-call(bf16[32,24,128]{2,1,0:T(8,128)(2,1)S(1)} %all-to-all-done.3.recv, f32[8,128]{1,0:T(8,128)S(1)} %get-tuple-element.87.features, f32[144,128]{1,0:T(8,128)S(1)} %get-tuple-element.76.stats_one.stats, ...), custom_call_target="tpu_custom_call" | custom-call | flops 100000000 | bytes 4000000 | tf_op jit(solution)/shard_map/pallas_call | solution.py:937
  (1 shorter events, 0.0 us)
Async XLA Ops:
  2.7 15.3 %all-to-all-start = ((bf16[32,16,128]{2,1,0:T(8,128)(2,1)}), bf16[32,16,128]{2,1,0:T(8,128)(2,1)S(1)}, u32[]{:S(2)}, u32[]{:S(2)}) async-start(bf16[32,16,128]{2,1,0:T(8,128)(2,1)} %get-tuple-element.55), calls=%async_computation | async-start | bytes 262144 | tf_op jit(solution)/shard_map/all_to_all | solution.py:961
  31.8 1.7 %collective-permute-start = (f32[320,128]{1,0:T(8,128)S(1)}, f32[320,128]{1,0:T(8,128)S(1)}, u32[]{:S(2)}, u32[]{:S(2)}) collective-permute-start(f32[320,128]{1,0:T(8,128)S(1)} %get-tuple-element.72), channel_id=1, source_target_pairs={{0,1},{1,0},{2,3},{3,2},{4,5},{5,4},{6,7},{7,6},{8,9},{9,8},{10,11... | collective-permute-start | bytes 491528 | tf_op jit(solution)/shard_map/ppermute | solution.py:1088
  47.0 11.5 %all-to-all-start.3 = ((bf16[32,24,128]{2,1,0:T(8,128)(2,1)}), bf16[32,24,128]{2,1,0:T(8,128)(2,1)S(1)}, u32[]{:S(2)}, u32[]{:S(2)}) async-start(bf16[32,24,128]{2,1,0:T(8,128)(2,1)} %get-tuple-element.86), calls=%async_computation.3 | async-start | bytes 393216 | tf_op jit(solution)/shard_map/all_to_all | solution.py:961

commit v7 on v4

--- a/solution.py
+++ b/solution.py
@@ -568,8 +568,8 @@
         right[0:chan, lanes] = g.astype(BF16)
         right[chan : 2 * chan, lanes] = normed.astype(BF16)
         right[2 * chan : 3 * chan, lanes] = (g - right[0:chan, lanes].astype(F32)).astype(BF16)
-        if m in (5, 11, rows - 1):
-            start = m - m % 6
+        if m % 8 == 7:
+            start = m - 7
             left = [act[(n + 2) * 3 * chan : (n + 5) * 3 * chan, :frame_dev] for n in range(start, m + 1)]
             lanes = slice(start * frame_dev, (m + 1) * frame_dev)
             table = table + dot(jnp.concatenate(left, axis=1), right[:, lanes], ((1,), (1,)))

time: 60.3 us -> 60.3 us (level)
  no operation moved by 1% of the time
where the time goes in v7:
time: 60.3 us; the launch traced here: 60 us
  blocking collectives  19.5 us (32%)
  Pallas kernels  18 us (30%)
  waiting for transfers between devices  11.9 us (20%)
  starting transfers between devices  9.87 us (16%)
  between operations  0.7 us (1%)
    all_to_all x2, blocking collectives, exchange(): return lax.all_to_all(blocks, axes, 0, 0, tiled=True)  19.5 us
    pallas_call x10, Pallas kernels, run(): pl.pallas_call(kernel, out_shape=outs, in_specs=specs, out_specs=[pl.Bloc...  18 us
    all_to_all x2, waiting for transfers between devices, exchange(): return lax.all_to_all(blocks, axes, 0, 0, tiled=True)  11.9 us
    all_to_all x2, starting transfers between devices, exchange(): return lax.all_to_all(blocks, axes, 0, 0, tiled=True)  9.42 us
  transfers between devices with their start and end apart: 3, of which 2 were waited for; matrix products, arithmetic and copies ran while one was open for 0% of the time, Pallas kernels for 11%

profile of v7, /device:TPU:1, one launch (start us, length us, event | category | flops | bytes accessed | tf_op | source)
XLA Modules:
  0.0 60.0 jit_solution(13634767916654385069)
XLA Ops:
  0.6 2.1 %shard_map.152 = (bf16[32,16,128]{2,1,0:T(8,128)(2,1)}, bf16[1,64,8,128]{3,2,1,0:T(8,128)(2,1)S(1)}, bf16[1,16,256]{2,1,0:T(8,128)(2,1)S(1)}, f32[8,384]{1,0:T(8,128)S(1)}) custom-call(bf16[1,16,256]{2,1,0:T(8,128)(2,1)} %spec_hbm.1, bf16[1,64,8,128]{3,2,1,0:T(8,128)(2,1)} %grad_hbm.1, s32[1,4]{1,0:T(1,128)} %bounds_hbm.3), custom_call_target="tpu_custom_call" | custom-call | flops 100000000 | bytes 4000000 | tf_op jit(solution)/shard_map/pallas_call | solution.py:933
  2.7 7.1 %all-to-all-start = ((bf16[32,16,128]{2,1,0:T(8,128)(2,1)}), bf16[32,16,128]{2,1,0:T(8,128)(2,1)S(1)}, u32[]{:S(2)}, u32[]{:S(2)}) async-start(bf16[32,16,128]{2,1,0:T(8,128)(2,1)} %get-tuple-element.55), calls=%async_computation | async-start | bytes 262144 | tf_op jit(solution)/shard_map/all_to_all | solution.py:957
  9.8 2.0 %shard_map.153 = (bf16[128,768]{1,0:T(8,128)(2,1)S(1)}, bf16[128,768]{1,0:T(8,128)(2,1)S(1)}, bf16[1408,128]{1,0:T(8,128)(2,1)S(1)}, bf16[48,1152]{1,0:T(8,128)(...) custom-call(bf16[1,64,8,128]{3,2,1,0:T(8,128)(2,1)S(1)} %get-tuple-e, ...), custom_call_target="tpu_custom_call" | custom-call | flops 100000000 | bytes 4000000 | tf_op jit(solution)/shard_map/pallas_call | solution.py:933
  11.8 6.2 %all-to-all-done.recv = bf16[32,16,128]{2,1,0:T(8,128)(2,1)S(1)} async-done(((bf16[32,16,128]{2,1,0:T(8,128)(2,1)}), bf16[32,16,128]{2,1,0:T(8,128)(2,1)S(1)}, u32[]{:S(2)}, u32[]{:S(2)}) %all-to-all-start) | async-done | bytes 131104 | tf_op jit(solution)/shard_map/all_to_all | solution.py:957
  18.1 2.5 %shard_map.154 = (f32[1024,384]{1,0:T(8,128)S(1)}, bf16[32,8,128]{2,1,0:T(8,128)(2,1)S(1)}, bf16[4224,384]{1,0:T(8,128)(2,1)S(1)}, bf16[128,384]{1,0:T(8,128)(2,...) custom-call(bf16[32,16,128]{2,1,0:T(8,128)(2,1)S(1)} %all-to-all-done.recv, ...), custom_call_target="tpu_custom_call" | custom-call | flops 100000000 | bytes 4000000 | tf_op jit(solution)/shard_map/pallas_call | solution.py:933
  20.6 8.9 %all_to_all.20.recv = bf16[32,8,128]{2,1,0:T(8,128)(2,1)S(1)} all-to-all(bf16[32,8,128]{2,1,0:T(8,128)(2,1)S(1)} %get-tuple-element.67), channel_id=1, replica_groups=mesh['mel'=4,'tm'=8] {'mel','tm'}, dimensions={0} | all-to-all | bytes 131072 | tf_op jit(solution)/shard_map/all_to_all | solution.py:957
  29.5 2.4 %shard_map.155 = (f32[1024,256]{1,0:T(8,128)S(1)}, f32[320,128]{1,0:T(8,128)S(1)}, f32[320,128]{1,0:T(8,128)S(1)}, f32[8,128]{1,0:T(8,128)S(1)}, f32[72,128]{1,0:T(8,128)S(1)}, /*index=5*/f32[512,256]{1,0:T(8,128)S(1)}) custom-call(bf16[32,8,128]{2,1,0:T(8,128)(2,1)S(1)} %all_to_all.20.recv, f32[1024,384]{1,0:T(8,128)S(1)} %get-tuple-element.68.pre_two, ...), custom_call_target="tpu_custom_call" | custom-call | flops 100000000 | bytes 4000000 | tf_op jit(solution)/shard_map/pallas_call | solution.py:933
  31.9 0.4 collective-permute-start
  32.3 1.2 %shard_map.156 = (f32[256,384]{1,0:T(8,128)S(1)}, f32[256,384]{1,0:T(8,128)S(1)}, f32[1024,128]{1,0:T(8,128)S(1)}) custom-call(bf16[32,8,128]{2,1,0:T(8,128)(2,1)S(1)} %all_to_all.20.recv, f32[1024,384]{1,0:T(8,128)S(1)} %get-tuple-element.68.pre_two, bf16[4224,384]{1,0:T(8,128)(2,1)S(1)} %get-tuple-element.69.act, ...), custom_call_target="tpu_custom_call" | custom-call | flops 100000000 | bytes 4000000 | tf_op jit(solution)/shard_map/pallas_call | solution.py:933
  33.5 0.0 collective-permute-done.received
  33.6 10.6 %all_to_all.21 = f32[352,1,128]{2,1,0:T(1,128)S(1)} all-to-all(f32[352,1,128]{2,1,0:T(1,128)S(1)} %bitcast.21), channel_id=1, replica_groups=mesh['mel'=4,'tm'=8] {'mel','tm'}, dimensions={0} | all-to-all | bytes 360448 | tf_op jit(solution)/shard_map/all_to_all | solution.py:957
  44.2 2.9 %shard_map.158 = (bf16[1280,384]{1,0:T(8,128)(2,1)S(1)}, bf16[1024,256]{1,0:T(8,128)(2,1)S(1)}, bf16[32,24,128]{2,1,0:T(8,128)(2,1)}, f32[8,128]{1,0:T(8,128)S(1)}) custom-call(f32[352,128]{1,0:T(8,128)S(1)} %bitcast.20, f32[1024,384]{1,0:T(8,128)S(1)} %get-tuple-element.68.pre_two, f32[256,384]{1,0:T(8,128)S(1)} %get-tuple-element.79.pre_ring, ...), custom_call_target="tpu_custom_call" | custom-call | flops 100000000 | bytes 4000000 | tf_op jit(solution)/shard_map/pallas_call | solution.py:933
  47.1 2.3 %all-to-all-start.3 = ((bf16[32,24,128]{2,1,0:T(8,128)(2,1)}), bf16[32,24,128]{2,1,0:T(8,128)(2,1)S(1)}, u32[]{:S(2)}, u32[]{:S(2)}) async-start(bf16[32,24,128]{2,1,0:T(8,128)(2,1)} %get-tuple-element.86), calls=%async_computation.3 | async-start | bytes 393216 | tf_op jit(solution)/shard_map/all_to_all | solution.py:957
  49.4 1.3 %shard_map.159 = (bf16[1,64,8,128]{3,2,1,0:T(8,128)(2,1)}, f32[1,64]{1,0:T(1,128)}, f32[1,64]{1,0:T(1,128)}) custom-call(f32[8,128]{1,0:T(8,128)S(1)} %get-tuple-element.83.totals, f32[512,256]{1,0:T(8,128)S(1)} %get-tuple-element.84.pairs), custom_call_target="tpu_custom_call" | custom-call | flops 100000000 | bytes 4000000 | tf_op jit(solution)/shard_map/pallas_call | solution.py:933
  50.7 2.2 %shard_map.160 = (f32[48,384]{1,0:T(8,128)S(1)}, bf16[48,1152]{1,0:T(8,128)(2,1)S(1)}, f32[32,64]{1,0:T(8,128)S(1)}) custom-call(bf16[1280,384]{1,0:T(8,128)(2,1)S(1)} %get-tuple-element.89.grad, bf16[1024,256]{1,0:T(8,128)(2,1)S(1)} %get-tuple-element.90.own_low, bf16[1408,128]{1,0:T(8,128)(2,1)S(1)} %get-tuple-element.61.w1, ...), custom_call_target="tpu_custom_call" | custom-call | flops 100000000 | bytes 4000000 | tf_op jit(solution)/shard_map/pallas_call | solution.py:933
  52.9 5.7 %all-to-all-done.3.recv = bf16[32,24,128]{2,1,0:T(8,128)(2,1)S(1)} async-done(((bf16[32,24,128]{2,1,0:T(8,128)(2,1)}), bf16[32,24,128]{2,1,0:T(8,128)(2,1)S(1)}, u32[]{:S(2)}, u32[]{:S(2)}) %all-to-all-start.3) | async-done | bytes 196640 | tf_op jit(solution)/shard_map/all_to_all | solution.py:957
  58.5 1.5 %shard_map.161 = (f32[1,16,256]{2,1,0:T(8,128)}, f32[3,3,64]{2,1,0:T(4,128)}, f32[9,64,64]{2,1,0:T(8,128)}, f32[1,64]{1,0:T(1,128)}, f32[1,64]{1,0:T(1,128)}) custom-call(bf16[32,24,128]{2,1,0:T(8,128)(2,1)S(1)} %all-to-all-done.3.recv, f32[8,128]{1,0:T(8,128)S(1)} %get-tuple-element.87.features, f32[144,128]{1,0:T(8,128)S(1)} %get-tuple-element.76.stats_one.stats, ...), custom_call_target="tpu_custom_call" | custom-call | flops 100000000 | bytes 4000000 | tf_op jit(solution)/shard_map/pallas_call | solution.py:933
  (1 shorter events, 0.0 us)
Async XLA Ops:
  2.7 15.3 %all-to-all-start = ((bf16[32,16,128]{2,1,0:T(8,128)(2,1)}), bf16[32,16,128]{2,1,0:T(8,128)(2,1)S(1)}, u32[]{:S(2)}, u32[]{:S(2)}) async-start(bf16[32,16,128]{2,1,0:T(8,128)(2,1)} %get-tuple-element.55), calls=%async_computation | async-start | bytes 262144 | tf_op jit(solution)/shard_map/all_to_all | solution.py:957
  31.9 1.7 %collective-permute-start = (f32[320,128]{1,0:T(8,128)S(1)}, f32[320,128]{1,0:T(8,128)S(1)}, u32[]{:S(2)}, u32[]{:S(2)}) collective-permute-start(f32[320,128]{1,0:T(8,128)S(1)} %get-tuple-element.72), channel_id=1, source_target_pairs={{0,1},{1,0},{2,3},{3,2},{4,5},{5,4},{6,7},{7,6},{8,9},{9,8},{10,11... | collective-permute-start | bytes 491528 | tf_op jit(solution)/shard_map/ppermute | solution.py:1084
  47.1 11.5 %all-to-all-start.3 = ((bf16[32,24,128]{2,1,0:T(8,128)(2,1)}), bf16[32,24,128]{2,1,0:T(8,128)(2,1)S(1)}, u32[]{:S(2)}, u32[]{:S(2)}) async-start(bf16[32,24,128]{2,1,0:T(8,128)(2,1)} %get-tuple-element.86), calls=%async_computation.3 | async-start | bytes 393216 | tf_op jit(solution)/shard_map/all_to_all | solution.py:957
